TPU v7x, 256 devices: a whole 4x4x8 slice. The times are simulated.
256 devices in a mesh: row: 8 (over x, core), col: 32 (over z, y).
Axes of the slice: x: 4, y: 4, z: 8, core: 2. Of those that a mesh axis runs over, the one named last changes fastest.
Arguments:
- x_saved: bfloat16 [2048, 6144], P('col', 'row'), may hold values from -1.59375 to 1.59375
- out_grad: bfloat16 [2048, 6144], P('col', 'row'), may hold values from -2 to 2
- hidden_pre: bfloat16 [2048, 24576], P('row', 'col'), may hold values from -6 to 6
- w_in: bfloat16 [6144, 24576], P('row', 'col'), may hold values from -0.078125 to 0.078125
- w_out: bfloat16 [24576, 6144], P('col', 'row'), may hold values from -0.0390625 to 0.0390625
Outputs:
- grad_x: bfloat16 [2048, 6144], P('col', 'row')
- grad_w_in: float32 [6144, 24576], P('row', 'col')
- grad_w_out: float32 [24576, 6144], P('col', 'row')
All inputs are finite; a program needn't handle non-finite values.
Results may differ from a plain program's by a relative error of at most 0.0049.
Values may be sent and summed in bfloat16 or wider, within the bound.
No kernel may reach another device: no remote copies, remote signals or barrier semaphores. Data moves between devices by JAX's collectives and lax.ppermute only.
A program may use at most 128 MiB of HBM per device.

v0:
```python
import jax
import jax.numpy as jnp
from jax import lax
from jax.sharding import PartitionSpec as P

coef = 0.7978845608
cubic = 0.044715


def gelu_value(h):
    t = jnp.tanh(coef * (h + cubic * h * h * h))
    return 0.5 * h * (1.0 + t)


def gelu_slope(h):
    t = jnp.tanh(coef * (h + cubic * h * h * h))
    return 0.5 * (1.0 + t) + 0.5 * h * (1.0 - t * t) * coef * (1.0 + 3.0 * cubic * h * h)


def right_product(left, right):
    return lax.dot_general(
        left, right, (((1,), (1,)), ((), ())), preferred_element_type=jnp.float32
    )


def token_product(left, right):
    return lax.dot_general(
        left, right, (((0,), (0,)), ((), ())), preferred_element_type=jnp.float32
    )


def local(x_saved, out_grad, hidden_pre, w_in, w_out):
    inputs_all, cotan_all = (
        lax.all_gather(x_saved, "col", axis=0, tiled=True),
        lax.all_gather(out_grad, "col", axis=0, tiled=True),
    )
    act_grad = lax.psum(right_product(cotan_all, w_out), "row")
    pre_all = lax.all_gather(hidden_pre, "row", axis=0, tiled=True).astype(jnp.float32)
    pre_grad_all = (act_grad * gelu_slope(pre_all)).astype(jnp.bfloat16)
    activated_all = gelu_value(pre_all).astype(jnp.bfloat16)
    grad_x = lax.psum_scatter(
        right_product(pre_grad_all, w_in), "col", scatter_dimension=0, tiled=True
    ).astype(jnp.bfloat16)
    grad_w_in = token_product(inputs_all, pre_grad_all)
    grad_w_out = token_product(activated_all, cotan_all)
    return (grad_x, grad_w_in, grad_w_out)


def solution(mesh):
    placed = (P("col", "row"), P("col", "row"), P("row", "col"), P("row", "col"), P("col", "row"))
    return jax.shard_map(
        local,
        mesh=mesh,
        in_specs=placed,
        out_specs=(P("col", "row"), P("row", "col"), P("col", "row")),
        check_vma=False,
    )
```

profile of v0, /device:TPU:8, one launch (start us, length us, event | category | flops | bytes accessed | tf_op | source)
XLA Modules:
  0.0 528.6 jit_solution(8004294094777284603)
XLA Ops:
  7.2 0.0 copy-start
  7.2 0.0 all-gather.4.cloned.1.call-start
  7.2 0.7 all-gather.4.cloned.1.call-update
  7.9 0.0 all-gather.6.cloned.1.call-start
  8.0 0.7 all-gather.6.cloned.1.call-update
  8.7 0.0 all-reduce.2.cloned.1.call-start
  8.7 83.5 %all-gather.4.cloned.1.call-done = bf16[2048,768]{1,0:T(8,128)(2,1)} async-done(((bf16[64,768]{1,0:T(8,128)(2,1)}), bf16[2048,768]{1,0:T(8,128)(2,1)}) %all-gather.4.cloned.1.call-update) | async-done | bytes 3145744 | tf_op jit(solution)/shard_map/all_gather | solution.py:35
  92.2 0.0 copy-done
  92.2 7.2 %fusion.17 = f32[2048,768]{1,0:T(8,128)} fusion(bf16[2048,768]{1,0:T(8,128)(2,1)} %all-gather.4.cloned.1.call-done, bf16[768,768]{1,0:T(8,128)(2,1)S(1)} %copy-done), kind=kOutput, calls=%fused_computation.24 | convolution fusion | flops 2415919104 | bytes 10616832 | tf_op jit(solution)/shard_map/dot_general | solution.py:21
  99.4 0.0 all-reduce.2.cloned.1.call-update
  99.4 0.0 all-gather.8.cloned.1.call-start
  99.5 0.5 all-gather.8.cloned.1.call-update
  100.0 0.0 copy-start.2
  100.0 0.2 reduce-scatter.2.cloned.1.call-start
  100.2 22.0 %all-gather.6.cloned.1.call-done = bf16[2048,768]{1,0:T(8,128)(2,1)} async-done(((bf16[256,768]{1,0:T(8,128)(2,1)}), bf16[2048,768]{1,0:T(8,128)(2,1)}) %all-gather.6.cloned.1.call-update) | async-done | bytes 3145744 | tf_op jit(solution)/shard_map/all_gather | solution.py:38
  122.2 91.8 %all-reduce.2.cloned.1.call-done = f32[2048,768]{1,0:T(8,128)} async-done(((f32[2048,768]{1,0:T(8,128)}), f32[2048,768]{1,0:T(8,128)}) %all-reduce.2.cloned.1.call-update) | async-done | bytes 6291472 | tf_op jit(solution)/shard_map/psum | solution.py:37
  214.0 6.5 %fusion.6 = bf16[2048,768]{1,0:T(8,128)(2,1)S(1)} fusion(f32[2048,768]{1,0:T(8,128)} %all-reduce.2.cloned.1.call-done, bf16[2048,768]{1,0:T(8,128)(2,1)} %all-gather.6.cloned.1.call-done), kind=kLoop, calls=%fused_computation.13 | loop fusion | flops 31457280 | bytes 12582912 | tf_op jit(solution)/shard_map/convert_element_type | solution.py:39
  220.6 0.0 copy-start.1
  220.6 1.7 copy-done.1
  222.3 0.0 copy-done.2
  222.3 4.5 fusion.18
  226.8 0.0 reduce-scatter.2.cloned.1.call-update
  226.8 7.8 %fusion.11 = f32[768,768]{1,0:T(8,128)} fusion(bf16[2048,768]{1,0:T(8,128)(2,1)} %all-gather.4.cloned.1.call-done, bf16[2048,768]{1,0:T(8,128)(2,1)} %all-gather.6.cloned.1.call-done), kind=kOutput, calls=%fused_computation.18 | convolution fusion | flops 2431647744 | bytes 8650752 | tf_op jit(solution)/shard_map/dot_general | solution.py:27
  234.6 60.4 %all-gather.8.cloned.1.call-done = bf16[2048,768]{1,0:T(8,128)(2,1)} async-done(((bf16[64,768]{1,0:T(8,128)(2,1)}), bf16[2048,768]{1,0:T(8,128)(2,1)}) %all-gather.8.cloned.1.call-update) | async-done | bytes 3145744 | tf_op jit(solution)/shard_map/all_gather | solution.py:34
  295.0 5.5 %convolution_bitcast_fusion = f32[768,768]{0,1:T(8,128)S(1)} fusion(bf16[2048,768]{1,0:T(8,128)(2,1)} %copy-done.1, bf16[2048,768]{1,0:T(8,128)(2,1)} %all-gather.8.cloned.1.call-done), kind=kOutput, calls=%fused_computation.19 | convolution fusion | flops 2415919104 | bytes 8650752 | tf_op jit(solution)/shard_map/dot_general | solution.py:27
  300.5 2.0 copy.8
  302.5 218.0 %reduce-scatter.2.cloned.1.call-done = f32[64,768]{1,0:T(8,128)} async-done(((f32[2048,768]{1,0:T(8,128)}), f32[64,768]{1,0:T(8,128)}) %reduce-scatter.2.cloned.1.call-update) | async-done | bytes 196624 | tf_op jit(solution)/shard_map/reduce_scatter | solution.py:41
  520.5 1.6 convert_element_type.14
Async XLA Ops:
  7.2 85.1 %copy-start = (bf16[768,768]{1,0:T(8,128)(2,1)S(1)}, bf16[768,768]{1,0:T(8,128)(2,1)}, u32[]{:S(2)}) copy-start(bf16[768,768]{1,0:T(8,128)(2,1)} %param.9) | copy-start | bytes 3538948
  7.2 85.0 %all-gather.4.cloned.1.call-start = ((), (), s32[]{:S(2)}) async-start(), calls=%async_computation.1 | async-start | bytes 3244032 | tf_op jit(solution)/shard_map/all_gather | solution.py:35
  7.9 114.3 %all-gather.6.cloned.1.call-start = ((), (), s32[]{:S(2)}) async-start(), calls=%async_computation.3 | async-start | bytes 3538944 | tf_op jit(solution)/shard_map/all_gather | solution.py:38
  8.7 205.3 %all-reduce.2.cloned.1.call-start = ((), (), s32[]{:S(2)}) async-start(), calls=%async_computation.2 | async-start | bytes 12582912 | tf_op jit(solution)/shard_map/psum | solution.py:37
  99.4 195.6 %all-gather.8.cloned.1.call-start = ((), (), s32[]{:S(2)}) async-start(), calls=%async_computation.5 | async-start | bytes 3244032 | tf_op jit(solution)/shard_map/all_gather | solution.py:34
  100.0 122.3 %copy-start.2 = (bf16[768,768]{1,0:T(8,128)(2,1)S(1)}, bf16[768,768]{1,0:T(8,128)(2,1)}, u32[]{:S(2)}) copy-start(bf16[768,768]{1,0:T(8,128)(2,1)} %param.8) | copy-start | bytes 3538948
  100.0 420.5 %reduce-scatter.2.cloned.1.call-start = ((), (), s32[]{:S(2)}) async-start(), calls=%async_computation.4 | async-start | bytes 6488064 | tf_op jit(solution)/shard_map/reduce_scatter | solution.py:41
  220.6 1.7 copy-start.1
Sparse Core Ops, SparseCore 0:
  10.6 81.5 all-gather.3
  94.1 28.1 all-gather.5
  124.6 89.3 all-reduce.1
  216.4 78.5 all-gather.7
  298.8 221.6 reduce-scatter.1
where the time goes:
time: 530 us; the launch traced here: 529 us
  waiting for transfers between devices  478 us (90%)
  matrix products  25 us (5%)
  between operations  13.8 us (3%)
  other arithmetic  8.13 us (2%)
    reduce_scatter x1, waiting for transfers between devices, local(): lax.psum_scatter(right_product(pre_grad_all, w_in), 'col', scatter_dimens...  218 us
    psum x1, waiting for transfers between devices, local(): act_grad = lax.psum(right_product(cotan_all, w_out), 'row')  91.8 us
    all_gather x1, waiting for transfers between devices, local(): lax.all_gather(out_grad, 'col', axis=0, tiled=True)  83.5 us
    all_gather x1, waiting for transfers between devices, local(): lax.all_gather(x_saved, 'col', axis=0, tiled=True)  60.4 us
    all_gather x1, waiting for transfers between devices, local(): lax.all_gather(hidden_pre, 'row', axis=0, tiled=True).astype(jnp.float32)  22 us
    dot_general x2, matrix products, token_product(): lax.dot_general(left, right, (((0,), (0,)), ((), ())), preferred_element_...  13.3 us
    dot_general x2, matrix products, right_product(): lax.dot_general(left, right, (((1,), (1,)), ((), ())), preferred_element_...  11.7 us
  transfers between devices with their start and end apart: 5, of which 5 were waited for; matrix products, arithmetic and copies ran while one was open for 6% of the time, Pallas kernels for 0%

commit v1 on v0

v1 whole, which is shorter than its diff:
```python
import functools

import jax
import jax.numpy as jnp
from jax import lax
from jax.experimental import pallas as pl
from jax.experimental.pallas import tpu as pltpu
from jax.sharding import Mesh, PartitionSpec as P

coef = 0.7978845608
cubic = 0.044715

NX, NC, NZ, NY = 4, 2, 8, 4
ROWS, HALF, SHARD = 256, 32, 64
BF = jnp.bfloat16
F32 = jnp.float32
GROUPS = ((0, 1, -1, 2, -2), (3, -3, 4))
ORDER = tuple(s for group in GROUPS for s in group)
BACK = ((4, -3, 3, -2), (2, -1, 1, 0))
FEATURES = 768
LIMIT = 48 * 1024 * 1024


def shift(a, axis, by):
    n = lax.axis_size(axis)
    return lax.ppermute(a, axis, [(i, (i + by) % n) for i in range(n)])


def token_product(left, right):
    return lax.dot_general(left, right, (((0,), (0,)), ((), ())), preferred_element_type=F32)


def right_product(left, right):
    return lax.dot_general(left, right, (((1,), (1,)), ((), ())), preferred_element_type=F32)


def call(body, pos, args, outs, name, flops=0, scratch=(), space=pltpu.VMEM):
    return pl.pallas_call(
        body,
        in_specs=[pl.BlockSpec(memory_space=pltpu.SMEM)]
        + [pl.BlockSpec(memory_space=None if a.shape[0] == FEATURES else space) for a in args],
        out_specs=[pl.BlockSpec(memory_space=pltpu.VMEM)] * len(outs),
        out_shape=outs,
        scratch_shapes=list(scratch),
        compiler_params=pltpu.CompilerParams(vmem_limit_bytes=LIMIT),
        cost_estimate=pl.CostEstimate(flops=1, bytes_accessed=1, transcendentals=0),
        name=name,
    )(pos, *args)


def shape(dtype, *dims):
    return jax.ShapeDtypeStruct(dims, dtype)


def tokens_at(block, half):
    return pl.ds(pl.multiple_of(block * SHARD + half * HALF, HALF), HALF)


def after(a, token):
    if token is None:
        return a
    return lax.optimization_barrier((a, token))[0]


def together(*arrays):
    return list(lax.optimization_barrier(arrays))


def slab_of(shard):
    return jnp.concatenate([shard, shift(shard, "y", -1), shift(shard, "y", 2), shift(shard, "y", 1)])


def slab_start(pos, s, j):
    return lax.rem(pos[3] + (s + NZ), NZ) * ROWS + lax.rem(pos[2] + j, NY) * SHARD


def w_out_kernel(pos, hid_ref, *refs):
    *slabs, out_ref, held = refs
    for i, (s, slab) in enumerate(zip(ORDER, slabs)):
        for j in range(NY):
            start = pl.multiple_of(slab_start(pos, s, j), SHARD)
            v = hid_ref[pl.ds(start, SHARD), :].astype(F32)
            t = jnp.tanh(coef * (v + cubic * v * v * v))
            held[j * SHARD : (j + 1) * SHARD, :] = (0.5 * v * (1.0 + t)).astype(BF)
        term = token_product(held[...], slab[...])
        out_ref[...] = term if i == 0 else out_ref[...] + term


def w_in_kernel(pos, x_ref, *refs):
    *groups, out_ref, held = refs
    for g, group in enumerate(BACK):
        for n, s in enumerate(group):
            for j in range(NY):
                start = pl.multiple_of(slab_start(pos, s, j), SHARD)
                held[j * SHARD : (j + 1) * SHARD, :] = x_ref[pl.ds(start, SHARD), :]
            term = token_product(held[...], groups[g][n])
            out_ref[...] = term if g == n == 0 else out_ref[...] + term


def own_kernel(pos, hid_ref, t0, t1, t2, t3, *out_refs):
    for i, s in enumerate(ORDER):
        start = pl.multiple_of(slab_start(pos, s, pos[0]) + pos[1] * HALF, HALF)
        v = hid_ref[pl.ds(start, HALF), :].astype(F32)
        t = jnp.tanh(coef * (v + cubic * v * v * v))
        slope = 0.5 * (1.0 + t) + 0.5 * v * (1.0 - t * t) * coef * (1.0 + 3.0 * cubic * v * v)
        total = t0[i] + t1[i].astype(F32) + t2[i].astype(F32) + t3[i].astype(F32)
        for group, ref in zip(BACK, out_refs):
            if s in group:
                ref[group.index(s)] = (total * slope).astype(BF)


def act_kernel(q, pos, *refs):
    slabs, (w_ref, keep_ref, give_ref, acc_ref) = refs[:q], refs[q:]
    x, core = pos[0], pos[1]
    for i in range(q):
        acc_ref[...] = right_product(slabs[i][...], w_ref[...])
        for k in range(NX):
            block = lax.rem(x + k, NX)
            keep_ref[k, i] = acc_ref[tokens_at(block, core), :]
            give_ref[k, i] = acc_ref[tokens_at(block, 1 - core), :].astype(BF)


def fold_kernel(n, pos, *refs):
    keeps, gots, (own_ref, *sent_refs) = refs[:n], refs[n : 2 * n], refs[2 * n :]
    first = 0
    for keep_ref, got_ref in zip(keeps, gots):
        slabs = slice(first, first + keep_ref.shape[1])
        first += keep_ref.shape[1]
        own_ref[slabs] = keep_ref[0] + got_ref[0].astype(F32)
        for k in range(1, NX):
            sent_refs[k - 1][slabs] = (keep_ref[k] + got_ref[k].astype(F32)).astype(BF)


def stack_kernel(pos, *refs):
    for k in range(len(refs) - 1):
        refs[-1][k] = refs[k][...]


def out_kernel(pos, ours_ref, other_ref, w_ref, pre_ref, own_ref, s1, s2, s3, acc_ref):
    x, core = pos[0], pos[1]
    for i in range(pre_ref.shape[0]):
        for k in range(NX):
            block = lax.rem(x + k, NX)
            pre_ref[i, tokens_at(block, core), :] = ours_ref[k, i]
            pre_ref[i, tokens_at(block, 1 - core), :] = other_ref[k, i]
        acc_ref[...] = right_product(pre_ref[i], w_ref[...])
        for j, ref in enumerate((own_ref, s1, s2, s3)):
            ref[i] = acc_ref[j * SHARD : (j + 1) * SHARD, :].astype(ref.dtype)


def hop(up, down):
    return [shift(up.astype(BF), "z", 1), shift(down.astype(BF), "z", -1)]


def local(x_saved, out_grad, hidden_pre, w_in, w_out):
    x, core, z, y = (lax.axis_index(a).astype(jnp.int32) for a in ("x", "core", "z", "y"))
    pos = jnp.stack([x, core, y, z])
    width, cols = x_saved.shape[1], hidden_pre.shape[1]
    hidden = lax.all_gather(hidden_pre, ("x", "core"), axis=0, tiled=True)
    flops = 2 * ROWS * width * cols
    cotan = {0: slab_of(out_grad)}

    def ring_step(s):
        cotan[s], cotan[-s] = together(shift(cotan[s - 1], "z", -1), shift(cotan[1 - s], "z", 1))

    def over_x(own):
        return [shift(own, "x", -1), shift(own, "x", 2), shift(own, "x", 1)]

    def stack(own, came):
        (ours,) = call(
            stack_kernel, pos, [own, *came], [shape(BF, NX, own.shape[0], HALF, cols)], "stack_pre"
        )
        return ours

    def back(ours, other):
        q = ours.shape[1]
        return call(
            out_kernel,
            pos,
            [ours, other, w_in],
            [shape(BF, q, ROWS, cols), shape(F32, q, SHARD, width)] + [shape(BF, q, SHARD, width)] * (NY - 1),
            "grad_x_products",
            flops=flops * q,
            scratch=[pltpu.VMEM((ROWS, width), F32)],
        )

    def products(group):
        q = len(group)
        return call(
            functools.partial(act_kernel, q),
            pos,
            [cotan[s] for s in group] + [w_out],
            [shape(F32, NX, q, HALF, cols), shape(BF, NX, q, HALF, cols)],
            "act_products",
            flops=flops * q,
            space=None,
            scratch=[pltpu.VMEM((ROWS, cols), F32)],
        )

    ring_step(1)
    ring_step(2)
    inputs = lax.all_gather(after(x_saved, cotan[2]), ("z", "y"), axis=0, tiled=True)
    keep, give = products(GROUPS[0])
    ring_step(3)
    middle = ROWS // 2
    low, high, give = together(cotan[-3][:middle], cotan[3][middle:], give)
    low, high, got = together(shift(low, "z", 1), shift(high, "z", -1), shift(give, "core", 1))
    cotan[4] = jnp.concatenate([low, high])
    last_keep, give = products(GROUPS[1])
    own, *sent = call(
        functools.partial(fold_kernel, 2),
        pos,
        [keep, last_keep, got, shift(give, "core", 1)],
        [shape(F32, NZ, HALF, cols)] + [shape(BF, NZ, HALF, cols)] * (NX - 1),
        "fold",
    )
    (grad_w_out,) = call(
        w_out_kernel,
        pos,
        [after(hidden, own)] + [cotan[s] for s in ORDER],
        [shape(F32, cols, width)],
        "grad_w_out",
        flops=flops * NZ,
        space=None,
        scratch=[pltpu.VMEM((ROWS, cols), BF)],
    )
    *came, grad_w_out = together(*(shift(a, "x", k + 1) for k, a in enumerate(sent)), grad_w_out)
    own, own_last = call(
        own_kernel, pos, [hidden, own, *came], [shape(BF, len(g), HALF, cols) for g in BACK], "pre_grad"
    )
    *came, own_last = together(*over_x(own), own_last)
    ours = stack(own, came)
    pre, near, *sent = back(ours, shift(ours, "core", 1))
    one, two, three, own_last = together(*sent, own_last)
    *came, one, three, two = together(*over_x(own_last), shift(one, "y", 1), shift(three, "y", 3), two)
    ours = stack(own_last, came)
    ours, two = together(ours, two)
    pre_last, near_last, *last = back(ours, shift(ours, "core", 1))
    near = near + one.astype(F32) + three.astype(F32)
    two, one, three, last_two = together(shift(two, "y", 2), last[0], last[2], last[1])
    near = near + two.astype(F32)
    two = last_two
    b = {s: near[i] for i, s in enumerate(BACK[0])}
    up, down, one, two, three = together(b[4].astype(BF), b[-3].astype(BF), one, two, three)
    up, down, one, three = together(*hop(up, down), shift(one, "y", 1), shift(three, "y", 3))
    up, down = up.astype(F32) + b[3], down.astype(F32) + b[-2]
    up, down, two = together(up.astype(BF), down.astype(BF), two)
    (grad_w_in,) = call(
        w_in_kernel,
        pos,
        [inputs, pre, after(pre_last, up)],
        [shape(F32, width, cols)],
        "grad_w_in",
        flops=flops * NZ,
        space=None,
        scratch=[pltpu.VMEM((ROWS, width), BF)],
    )
    up, down, two, grad_w_in = together(*hop(up, down), shift(two, "y", 2), grad_w_in)
    near = near_last + one.astype(F32) + two.astype(F32) + three.astype(F32)
    b = {s: near[i] for i, s in enumerate(BACK[1])}
    up, down = together((up.astype(F32) + b[2]).astype(BF), (down.astype(F32) + b[-1]).astype(BF))
    up, down = together(*hop(up, down))
    up = shift((up.astype(F32) + b[1]).astype(BF), "z", 1)
    grad_x = (b[0] + up.astype(F32) + down.astype(F32)).astype(BF)
    return (grad_x, grad_w_in, grad_w_out)


def solution(mesh):
    grid = Mesh(mesh.devices.reshape(NX, NC, NZ, NY), ("x", "core", "z", "y"))
    row, col = ("x", "core"), ("z", "y")
    return jax.shard_map(
        local,
        mesh=grid,
        in_specs=(P(col, row), P(col, row), P(row, col), P(row, col), P(col, row)),
        out_specs=(P(col, row), P(row, col), P(col, row)),
        check_vma=False,
    )
```

time: 530 us -> 208 us (0.39)
  waiting for transfers between devices: 478 us -> 86.9 us
  starting transfers between devices: 0.37 us -> 66.9 us
  Pallas kernels: 0 us -> 29.5 us
  matrix products: 25 us -> 0 us
    reduce_scatter x1 -> x0, waiting for transfers between devices: 218 us -> none  [local(): lax.psum_scatter(right_product(pre_grad_all, w_in), 'col', scatter_dimens...]
    all_gather x3 -> x2, waiting for transfers between devices: 166 us -> 0.01 us  [the longest x1 0.01 us: local(): hidden = lax.all_gather(hidden_pre, ('x', 'core'), axis=0, tiled=True)]
    psum x1 -> x0, waiting for transfers between devices: 91.8 us -> none  [local(): act_grad = lax.psum(right_product(cotan_all, w_out), 'row')]
    ppermute x0 -> x37, waiting for transfers between devices: none -> 86.2 us  [shift(): return lax.ppermute(a, axis, [(i, (i + by) % n) for i in range(n)])]
    ppermute x0 -> x37, starting transfers between devices: none -> 66.8 us  [shift(): return lax.ppermute(a, axis, [(i, (i + by) % n) for i in range(n)])]
    pallas_call x0 -> x10, Pallas kernels: none -> 29.5 us  [call(): pl.pallas_call(body, in_specs=[pl.BlockSpec(memory_space=pltpu.SMEM)] + [...]
    dot_general x4 -> x0, matrix products: 25 us -> none  [the longest x2 13.3 us: token_product(): lax.dot_general(left, right, (((0,), (0,)), ((), ())), preferred_element_...]
    convert_element_type x2 -> x4, other arithmetic: 8.13 us -> 2.45 us  [the longest x1 0.98 us: local(): (down.astype(F32) + b[-1]).astype(BF)]
  transfers between devices with their start and end apart: 5 -> 39, of which waited for: 5 -> 24; matrix products, arithmetic and copies ran while one was open for 6% -> 1% of each run, Pallas kernels for 0% -> 14%
where the time goes in v1:
time: 208 us; the launch traced here: 204 us
  waiting for transfers between devices  86.9 us (42%)
  starting transfers between devices  66.9 us (32%)
  Pallas kernels  29.5 us (14%)
  between operations  14.5 us (7%)
  other arithmetic  3.88 us (2%)
  local copies, waits for them, and re-layouts  2.35 us (1%)
    ppermute x37, waiting for transfers between devices, shift(): return lax.ppermute(a, axis, [(i, (i + by) % n) for i in range(n)])  86.2 us
    ppermute x37, starting transfers between devices, shift(): return lax.ppermute(a, axis, [(i, (i + by) % n) for i in range(n)])  66.8 us
    pallas_call x10, Pallas kernels, call(): pl.pallas_call(body, in_specs=[pl.BlockSpec(memory_space=pltpu.SMEM)] + [...  29.5 us
  transfers between devices with their start and end apart: 39, of which 24 were waited for; matrix products, arithmetic and copies ran while one was open for 1% of the time, Pallas kernels for 14%

profile of v1, /device:TPU:8, one launch (start us, length us, event | category | flops | bytes accessed | tf_op | source)
XLA Modules:
  0.0 204.0 jit_solution(3546331347049019450)
XLA Ops:
  7.2 0.7 all-gather.3.cloned.1.call-update
  8.0 2.3 %collective-permute-start = (bf16[64,768]{1,0:T(8,128)(2,1)}, bf16[64,768]{1,0:T(8,128)(2,1)S(1)}, u32[]{:S(2)}, u32[]{:S(2)}) collective-permute-start(bf16[64,768]{1,0:T(8,128)(2,1)} %param.6), channel_id=1, source_target_pairs={{0,3},{1,0},{2,1},{3,2},{4,7},{5,4},{6,5},{7,6},{8,11},{9,8},{10,9... | collective-permute-start | bytes 294920 | tf_op jit(solution)/shard_map/ppermute | solution.py:26
  10.2 0.9 collective-permute-start.1
  11.1 1.9 collective-permute-start.2
  13.0 0.9 constant_dynamic-update-slice_fusion.3
  13.9 2.6 %collective-permute-done.1 = bf16[64,768]{1,0:T(8,128)(2,1)S(1)} collective-permute-done((bf16[64,768]{1,0:T(8,128)(2,1)}, bf16[64,768]{1,0:T(8,128)(2,1)S(1)}, u32[]{:S(2)}, u32[]{:S(2)}) %collective-permute-start.1) | collective-permute-done | bytes 98336 | tf_op jit(solution)/shard_map/ppermute | solution.py:26
  16.7 5.9 %collective-permute-start.3 = (bf16[256,768]{1,0:T(8,128)(2,1)S(1)}, bf16[256,768]{1,0:T(8,128)(2,1)S(1)}, u32[]{:S(2)}, u32[]{:S(2)}) collective-permute-start(bf16[256,768]{1,0:T(8,128)(2,1)S(1)} %constant_dynamic-update-slice_fusion.refs_0_), channel_id=1, source_target_pairs={{0,28},{4,0},{8,4},{12,8},{16,12},{20,16},{24,20},{28,24},{1,29},{... | collective-permute-start | bytes 1179656 | tf_op jit(solution)/shard_map/ppermute | solution.py:26
  22.6 7.2 %collective-permute-done.3.refs_1_ = bf16[256,768]{1,0:T(8,128)(2,1)S(1)} collective-permute-done((bf16[256,768]{1,0:T(8,128)(2,1)S(1)}, bf16[256,768]{1,0:T(8,128)(2,1)S(1)}, u32[]{:S(2)}, u32[]{:S(2)}) %collective-permute-start.3) | collective-permute-done | bytes 393248 | tf_op jit(solution)/shard_map/ppermute | solution.py:26
  29.8 3.4 %collective-permute-done.4.refs_2_ = bf16[256,768]{1,0:T(8,128)(2,1)S(1)} collective-permute-done((bf16[256,768]{1,0:T(8,128)(2,1)S(1)}, bf16[256,768]{1,0:T(8,128)(2,1)S(1)}, u32[]{:S(2)}, u32[]{:S(2)}) %collective-permute-start.4) | collective-permute-done | bytes 393248 | tf_op jit(solution)/shard_map/ppermute | solution.py:26
  33.5 1.7 collective-permute-start.6
  35.2 6.5 %collective-permute-done.5.refs_3_ = bf16[256,768]{1,0:T(8,128)(2,1)S(1)} collective-permute-done((bf16[256,768]{1,0:T(8,128)(2,1)S(1)}, bf16[256,768]{1,0:T(8,128)(2,1)S(1)}, u32[]{:S(2)}, u32[]{:S(2)}) %collective-permute-start.5) | collective-permute-done | bytes 393248 | tf_op jit(solution)/shard_map/ppermute | solution.py:26
  41.8 1.5 collective-permute-done.6.refs_4_
  43.5 1.8 collective-permute-start.8
  45.4 2.9 %act_products.2 = (f32[4,5,32,768]{3,2,1,0:T(8,128)S(1)}, bf16[4,5,32,768]{3,2,1,0:T(8,128)(2,1)S(1)}) custom-call(s32[4]{0:T(128)S(1)} %pad_add_fusion.pos, bf16[256,768]{1,0:T(8,128)(2,1)S(1)} %constant_dynamic-update-slice_fusion.refs_0_, bf16[256,768]{1,0:T(8,128)(2,1)S(1)} %collective-permute-done.3.refs_1_, ...), custom_call_target="tpu_custom_call" | custom-call | flops 1 | bytes 1 | tf_op jit(solution)/shard_map/act_products/pallas_call | solution.py:38
  48.3 1.3 copy-done.3
  49.6 1.5 collective-permute-done.7.refs_0_.refs_5_
  51.1 1.6 collective-permute-done.8.refs_1_.refs_6_
  52.8 0.7 collective-permute-start.9
  53.5 2.6 %collective-permute-start.10 = (bf16[128,768]{1,0:T(8,128)(2,1)S(1)}, bf16[128,768]{1,0:T(8,128)(2,1)S(1)}, u32[]{:S(2)}, u32[]{:S(2)}) collective-permute-start(bf16[128,768]{1,0:T(8,128)(2,1)S(1)} %slice.33), channel_id=1, source_target_pairs={{0,28},{4,0},{8,4},{12,8},{16,12},{20,16},{24,20},{28,24},{1,29},{... | collective-permute-start | bytes 589832 | tf_op jit(solution)/shard_map/ppermute | solution.py:26
  56.1 5.2 %collective-permute-done.9 = bf16[128,768]{1,0:T(8,128)(2,1)S(1)} collective-permute-done((bf16[128,768]{1,0:T(8,128)(2,1)S(1)}, bf16[128,768]{1,0:T(8,128)(2,1)S(1)}, u32[]{:S(2)}, u32[]{:S(2)}) %collective-permute-start.9) | collective-permute-done | bytes 196640 | tf_op jit(solution)/shard_map/ppermute | solution.py:26
  61.4 1.7 act_products.3
  63.5 2.0 collective-permute-done.12.refs_3_
  65.5 2.8 %fold.1 = (f32[8,32,768]{2,1,0:T(8,128)S(1)}, bf16[8,32,768]{2,1,0:T(8,128)(2,1)}, bf16[8,32,768]{2,1,0:T(8,128)(2,1)}, bf16[8,32,768]{2,1,0:T(8,128)(2,1)}) custom-call(s32[4]{0:T(128)S(1)} %pad_add_fusion.pos, f32[4,5,32,768]{3,2,1,0:T(8,128)} %copy-done.3, f32[4,3,32,768]{3,2,1,0:T(8,128)S(1)} %get-tuple-element.95.refs_1_, ...), custom_call_target="tpu_custom_call" | custom-call | flops 1 | bytes 1 | tf_op jit(solution)/shard_map/fold/pallas_call | solution.py:38
  68.2 1.5 collective-permute-start.13
  69.7 2.8 %collective-permute-start.14 = (bf16[8,32,768]{2,1,0:T(8,128)(2,1)}, bf16[8,32,768]{2,1,0:T(8,128)(2,1)}, u32[]{:S(2)}, u32[]{:S(2)}) collective-permute-start(bf16[8,32,768]{2,1,0:T(8,128)(2,1)} %get-tuple-element.100), channel_id=1, source_target_pairs={{0,128},{64,192},{128,0},{192,64},{1,129},{65,193},{129,1},{193,65... | collective-permute-start | bytes 1179656 | tf_op jit(solution)/shard_map/ppermute | solution.py:26
  72.6 1.3 collective-permute-start.15
  73.9 7.0 %grad_w_out.1 = f32[768,768]{1,0:T(8,128)} custom-call(s32[4]{0:T(128)S(1)} %pad_add_fusion.pos, bf16[2048,768]{1,0:T(8,128)(2,1)} %all-gather.3.cloned.1.call-done.hid_ref, bf16[256,768]{1,0:T(8,128)(2,1)S(1)} %constant_dynamic-update-slice_fusion.refs_0_, bf16[256,768]{1,0:T(8,128)(2,1)S(1)} %collective-permute-done.3.refs_1_, ...), custom_call_target="tpu_custom_call" | custom-call | flops 1 | bytes 1 | tf_op jit(solution)/shard_map/grad_w_out/pallas_call | solution.py:38
  81.0 9.5 %collective-permute-done.14.t2 = bf16[8,32,768]{2,1,0:T(8,128)(2,1)} collective-permute-done((bf16[8,32,768]{2,1,0:T(8,128)(2,1)}, bf16[8,32,768]{2,1,0:T(8,128)(2,1)}, u32[]{:S(2)}, u32[]{:S(2)}) %collective-permute-start.14) | collective-permute-done | bytes 393248 | tf_op jit(solution)/shard_map/ppermute | solution.py:26
  90.5 1.9 pre_grad.1
  92.4 2.2 %collective-permute-start.16 = (bf16[4,32,768]{2,1,0:T(8,128)(2,1)S(1)}, bf16[4,32,768]{2,1,0:T(8,128)(2,1)S(1)}, u32[]{:S(2)}, u32[]{:S(2)}) collective-permute-start(bf16[4,32,768]{2,1,0:T(8,128)(2,1)S(1)} %get-tuple-element.106.refs_0_), channel_id=1, source_target_pairs={{0,192},{64,0},{128,64},{192,128},{1,193},{65,1},{129,65},{193,129... | collective-permute-start | bytes 589832 | tf_op jit(solution)/shard_map/ppermute | solution.py:26
  94.7 1.1 collective-permute-start.17
  95.8 0.7 collective-permute-start.18
  96.5 6.7 %collective-permute-done.16.refs_1_ = bf16[4,32,768]{2,1,0:T(8,128)(2,1)S(1)} collective-permute-done((bf16[4,32,768]{2,1,0:T(8,128)(2,1)S(1)}, bf16[4,32,768]{2,1,0:T(8,128)(2,1)S(1)}, u32[]{:S(2)}, u32[]{:S(2)}) %collective-permute-start.16) | collective-permute-done | bytes 196640 | tf_op jit(solution)/shard_map/ppermute | solution.py:26
  103.2 0.8 collective-permute-done.17.refs_2_
  104.0 2.8 %collective-permute-done.18.refs_3_ = bf16[4,32,768]{2,1,0:T(8,128)(2,1)S(1)} collective-permute-done((bf16[4,32,768]{2,1,0:T(8,128)(2,1)S(1)}, bf16[4,32,768]{2,1,0:T(8,128)(2,1)S(1)}, u32[]{:S(2)}, u32[]{:S(2)}) %collective-permute-start.18) | collective-permute-done | bytes 196640 | tf_op jit(solution)/shard_map/ppermute | solution.py:26
  107.5 2.3 %collective-permute-done.19.other_ref = bf16[4,4,32,768]{3,2,1,0:T(8,128)(2,1)S(1)} collective-permute-done((bf16[4,4,32,768]{3,2,1,0:T(8,128)(2,1)S(1)}, bf16[4,4,32,768]{3,2,1,0:T(8,128)(2,1)S(1)}, u32[]{:S(2)}, u32[]{:S(2)}) %collective-permute-start.19) | collective-permute-done | bytes 786464 | tf_op jit(solution)/shard_map/ppermute | solution.py:26
  109.7 3.0 %grad_x_products.2 = (bf16[4,256,768]{2,1,0:T(8,128)(2,1)}, f32[4,64,768]{2,1,0:T(8,128)S(1)}, bf16[4,64,768]{2,1,0:T(8,128)(2,1)S(1)}, bf16[4,64,768]{2,1,0:T(8,128)(2,1)S(1)}, bf16[4,64,768]{2,1,0:T(8,128)(2,1)S(1)}) custom-call(s32[4]{0:T(128)S(1)} %pad_add_fusion.pos, bf16[4,4,32,768]{3,2,1,0:T(8,128)(2,1)S(1)} %stack_pre.2.ours_ref, ...), custom_call_target="tpu_custom_call" | custom-call | flops 1 | bytes 1 | tf_op jit(solution)/shard_map/grad_x_products/pallas_call | solution.py:38
  112.7 1.6 collective-permute-start.23
  114.3 4.8 %collective-permute-start.24 = (bf16[4,64,768]{2,1,0:T(8,128)(2,1)S(1)}, bf16[4,64,768]{2,1,0:T(8,128)(2,1)S(1)}, u32[]{:S(2)}, u32[]{:S(2)}) collective-permute-start(bf16[4,64,768]{2,1,0:T(8,128)(2,1)S(1)} %get-tuple-element.117), channel_id=1, source_target_pairs={{0,3},{1,0},{2,1},{3,2},{4,7},{5,4},{6,5},{7,6},{8,11},{9,8},{10,9... | collective-permute-start | bytes 1179656 | tf_op jit(solution)/shard_map/ppermute | solution.py:26
  119.0 10.4 %collective-permute-start.20 = (bf16[4,32,768]{2,1,0:T(8,128)(2,1)S(1)}, bf16[4,32,768]{2,1,0:T(8,128)(2,1)S(1)}, u32[]{:S(2)}, u32[]{:S(2)}) collective-permute-start(bf16[4,32,768]{2,1,0:T(8,128)(2,1)S(1)} %get-tuple-element.115.refs_0_), channel_id=1, source_target_pairs={{0,192},{64,0},{128,64},{192,128},{1,193},{65,1},{129,65},{193,129... | collective-permute-start | bytes 589832 | tf_op jit(solution)/shard_map/ppermute | solution.py:26
  129.4 0.8 collective-permute-start.21
  130.1 0.8 collective-permute-start.22
  131.0 5.6 %collective-permute-done.20.refs_1_ = bf16[4,32,768]{2,1,0:T(8,128)(2,1)S(1)} collective-permute-done((bf16[4,32,768]{2,1,0:T(8,128)(2,1)S(1)}, bf16[4,32,768]{2,1,0:T(8,128)(2,1)S(1)}, u32[]{:S(2)}, u32[]{:S(2)}) %collective-permute-start.20) | collective-permute-done | bytes 196640 | tf_op jit(solution)/shard_map/ppermute | solution.py:26
  136.5 2.2 %collective-permute-done.21.refs_2_ = bf16[4,32,768]{2,1,0:T(8,128)(2,1)S(1)} collective-permute-done((bf16[4,32,768]{2,1,0:T(8,128)(2,1)S(1)}, bf16[4,32,768]{2,1,0:T(8,128)(2,1)S(1)}, u32[]{:S(2)}, u32[]{:S(2)}) %collective-permute-start.21) | collective-permute-done | bytes 196640 | tf_op jit(solution)/shard_map/ppermute | solution.py:26
  138.7 2.7 %collective-permute-done.22.refs_3_ = bf16[4,32,768]{2,1,0:T(8,128)(2,1)S(1)} collective-permute-done((bf16[4,32,768]{2,1,0:T(8,128)(2,1)S(1)}, bf16[4,32,768]{2,1,0:T(8,128)(2,1)S(1)}, u32[]{:S(2)}, u32[]{:S(2)}) %collective-permute-start.22) | collective-permute-done | bytes 196640 | tf_op jit(solution)/shard_map/ppermute | solution.py:26
  141.5 0.6 stack_pre.3.ours_ref
  142.2 2.2 %collective-permute-start.26 = (bf16[4,64,768]{2,1,0:T(8,128)(2,1)S(1)}, bf16[4,64,768]{2,1,0:T(8,128)(2,1)S(1)}, u32[]{:S(2)}, u32[]{:S(2)}) collective-permute-start(bf16[4,64,768]{2,1,0:T(8,128)(2,1)S(1)} %get-tuple-element.128), channel_id=1, source_target_pairs={{0,2},{1,3},{2,0},{3,1},{4,6},{5,7},{6,4},{7,5},{8,10},{9,11},{10,... | collective-permute-start | bytes 1179656 | tf_op jit(solution)/shard_map/ppermute | solution.py:26
  144.5 2.9 %grad_x_products.3 = (bf16[4,256,768]{2,1,0:T(8,128)(2,1)}, f32[4,64,768]{2,1,0:T(8,128)S(1)}, bf16[4,64,768]{2,1,0:T(8,128)(2,1)S(1)}, bf16[4,64,768]{2,1,0:T(8,128)(2,1)S(1)}, bf16[4,64,768]{2,1,0:T(8,128)(2,1)S(1)}) custom-call(s32[4]{0:T(128)S(1)} %pad_add_fusion.pos, bf16[4,4,32,768]{3,2,1,0:T(8,128)(2,1)S(1)} %stack_pre.3.ours_ref, ...), custom_call_target="tpu_custom_call" | custom-call | flops 1 | bytes 1 | tf_op jit(solution)/shard_map/grad_x_products/pallas_call | solution.py:38
  147.4 7.8 %collective-permute-done.26 = bf16[4,64,768]{2,1,0:T(8,128)(2,1)S(1)} collective-permute-done((bf16[4,64,768]{2,1,0:T(8,128)(2,1)S(1)}, bf16[4,64,768]{2,1,0:T(8,128)(2,1)S(1)}, u32[]{:S(2)}, u32[]{:S(2)}) %collective-permute-start.26) | collective-permute-done | bytes 393248 | tf_op jit(solution)/shard_map/ppermute | solution.py:26
  155.4 1.2 collective-permute-start.29
  156.6 1.9 collective-permute-start.30
  158.5 3.2 %collective-permute-start.28 = (bf16[64,768]{1,0:T(8,128)(2,1)S(1)}, bf16[64,768]{1,0:T(8,128)(2,1)S(1)}, u32[]{:S(2)}, u32[]{:S(2)}) collective-permute-start(bf16[64,768]{1,0:T(8,128)(2,1)S(1)} %get-tuple-element.137), channel_id=1, source_target_pairs={{0,28},{4,0},{8,4},{12,8},{16,12},{20,16},{24,20},{28,24},{1,29},{... | collective-permute-start | bytes 294920 | tf_op jit(solution)/shard_map/ppermute | solution.py:26
  161.8 2.6 %collective-permute-done.27 = bf16[64,768]{1,0:T(8,128)(2,1)S(1)} collective-permute-done((bf16[64,768]{1,0:T(8,128)(2,1)S(1)}, bf16[64,768]{1,0:T(8,128)(2,1)S(1)}, u32[]{:S(2)}, u32[]{:S(2)}) %collective-permute-start.27) | collective-permute-done | bytes 98336 | tf_op jit(solution)/shard_map/ppermute | solution.py:26
  164.4 3.0 %collective-permute-done.29 = bf16[4,64,768]{2,1,0:T(8,128)(2,1)S(1)} collective-permute-done((bf16[4,64,768]{2,1,0:T(8,128)(2,1)S(1)}, bf16[4,64,768]{2,1,0:T(8,128)(2,1)S(1)}, u32[]{:S(2)}, u32[]{:S(2)}) %collective-permute-start.29) | collective-permute-done | bytes 393248 | tf_op jit(solution)/shard_map/ppermute | solution.py:26
  167.4 0.8 fusion.10
  168.2 4.7 %collective-permute-start.33 = (bf16[4,64,768]{2,1,0:T(8,128)(2,1)S(1)}, bf16[4,64,768]{2,1,0:T(8,128)(2,1)}, u32[]{:S(2)}, u32[]{:S(2)}) collective-permute-start(bf16[4,64,768]{2,1,0:T(8,128)(2,1)S(1)} %get-tuple-element.146), channel_id=1, source_target_pairs={{0,2},{1,3},{2,0},{3,1},{4,6},{5,7},{6,4},{7,5},{8,10},{9,11},{10,... | collective-permute-start | bytes 1179656 | tf_op jit(solution)/shard_map/ppermute | solution.py:26
  172.9 3.2 %collective-permute-start.32 = (bf16[64,768]{1,0:T(8,128)(2,1)}, bf16[64,768]{1,0:T(8,128)(2,1)}, u32[]{:S(2)}, u32[]{:S(2)}) collective-permute-start(bf16[64,768]{1,0:T(8,128)(2,1)} %get-tuple-element.145), channel_id=1, source_target_pairs={{0,28},{4,0},{8,4},{12,8},{16,12},{20,16},{24,20},{28,24},{1,29},{... | collective-permute-start | bytes 294920 | tf_op jit(solution)/shard_map/ppermute | solution.py:26
  176.2 6.1 %grad_w_in.1 = f32[768,768]{1,0:T(8,128)} custom-call(s32[4]{0:T(128)S(1)} %pad_add_fusion.pos, bf16[2048,768]{1,0:T(8,128)(2,1)} %all-gather.5.cloned.1.call-done.x_ref, bf16[4,256,768]{2,1,0:T(8,128)(2,1)S(1)} %copy-done.6, bf16[4,256,768]{2,1,0:T(8,128)(2,1)S(1)} %copy-done.7), custom_call_target="tpu_custom_call" | custom-call | flops 1 | bytes 1 | tf_op jit(solution)/shard_map/grad_w_in/pallas_call | solution.py:38
  182.3 1.2 convert_add_fusion
  183.5 1.0 fusion.3
  184.6 3.2 %collective-permute-start.35 = (bf16[64,768]{1,0:T(8,128)(2,1)S(1)}, bf16[64,768]{1,0:T(8,128)(2,1)S(1)}, u32[]{:S(2)}, u32[]{:S(2)}) collective-permute-start(bf16[64,768]{1,0:T(8,128)(2,1)S(1)} %get-tuple-element.156), channel_id=1, source_target_pairs={{0,28},{4,0},{8,4},{12,8},{16,12},{20,16},{24,20},{28,24},{1,29},{... | collective-permute-start | bytes 294920 | tf_op jit(solution)/shard_map/ppermute | solution.py:26
  187.8 2.6 %collective-permute-done.34 = bf16[64,768]{1,0:T(8,128)(2,1)S(1)} collective-permute-done((bf16[64,768]{1,0:T(8,128)(2,1)S(1)}, bf16[64,768]{1,0:T(8,128)(2,1)S(1)}, u32[]{:S(2)}, u32[]{:S(2)}) %collective-permute-start.34) | collective-permute-done | bytes 98336 | tf_op jit(solution)/shard_map/ppermute | solution.py:26
  190.5 5.8 %collective-permute-done.36 = bf16[64,768]{1,0:T(8,128)(2,1)S(1)} collective-permute-done((bf16[64,768]{1,0:T(8,128)(2,1)S(1)}, bf16[64,768]{1,0:T(8,128)(2,1)S(1)}, u32[]{:S(2)}, u32[]{:S(2)}) %collective-permute-start.36) | collective-permute-done | bytes 98336 | tf_op jit(solution)/shard_map/ppermute | solution.py:26
  196.3 0.7 fusion.8
  (70 shorter events, 2.6 us)
Async XLA Ops:
  7.2 38.2 %copy-start.1 = (bf16[768,768]{1,0:T(8,128)(2,1)S(1)}, bf16[768,768]{1,0:T(8,128)(2,1)}, u32[]{:S(2)}) copy-start(bf16[768,768]{1,0:T(8,128)(2,1)} %refs_3_.1) | copy-start | bytes 3538948
  7.2 66.7 %all-gather.3.cloned.1.call-start = ((), (), s32[]{:S(2)}) async-start(), calls=%async_computation | async-start | bytes 3538944 | tf_op jit(solution)/shard_map/all_gather | solution.py:159
  7.9 168.2 %all-gather.5.cloned.1.call-start = ((), (), s32[]{:S(2)}) async-start(), calls=%async_computation.1 | async-start | bytes 3244032 | tf_op jit(solution)/shard_map/all_gather | solution.py:202
  8.0 5.9 %collective-permute-start = (bf16[64,768]{1,0:T(8,128)(2,1)}, bf16[64,768]{1,0:T(8,128)(2,1)S(1)}, u32[]{:S(2)}, u32[]{:S(2)}) collective-permute-start(bf16[64,768]{1,0:T(8,128)(2,1)} %param.6), channel_id=1, source_target_pairs={{0,3},{1,0},{2,1},{3,2},{4,7},{5,4},{6,5},{7,6},{8,11},{9,8},{10,9... | collective-permute-start | bytes 294920 | tf_op jit(solution)/shard_map/ppermute | solution.py:26
  10.2 6.3 %collective-permute-start.1 = (bf16[64,768]{1,0:T(8,128)(2,1)}, bf16[64,768]{1,0:T(8,128)(2,1)S(1)}, u32[]{:S(2)}, u32[]{:S(2)}) collective-permute-start(bf16[64,768]{1,0:T(8,128)(2,1)} %param.6), channel_id=1, source_target_pairs={{0,2},{1,3},{2,0},{3,1},{4,6},{5,7},{6,4},{7,5},{8,10},{9,11},{10,... | collective-permute-start | bytes 294920 | tf_op jit(solution)/shard_map/ppermute | solution.py:26
  11.1 5.6 %collective-permute-start.2 = (bf16[64,768]{1,0:T(8,128)(2,1)}, bf16[64,768]{1,0:T(8,128)(2,1)S(1)}, u32[]{:S(2)}, u32[]{:S(2)}) collective-permute-start(bf16[64,768]{1,0:T(8,128)(2,1)} %param.6), channel_id=1, source_target_pairs={{0,1},{1,2},{2,3},{3,0},{4,5},{5,6},{6,7},{7,4},{8,9},{9,10},{10,1... | collective-permute-start | bytes 294920 | tf_op jit(solution)/shard_map/ppermute | solution.py:26
  16.7 13.1 %collective-permute-start.3 = (bf16[256,768]{1,0:T(8,128)(2,1)S(1)}, bf16[256,768]{1,0:T(8,128)(2,1)S(1)}, u32[]{:S(2)}, u32[]{:S(2)}) collective-permute-start(bf16[256,768]{1,0:T(8,128)(2,1)S(1)} %constant_dynamic-update-slice_fusion.refs_0_), channel_id=1, source_target_pairs={{0,28},{4,0},{8,4},{12,8},{16,12},{20,16},{24,20},{28,24},{1,29},{... | collective-permute-start | bytes 1179656 | tf_op jit(solution)/shard_map/ppermute | solution.py:26
  22.6 10.6 %collective-permute-start.4 = (bf16[256,768]{1,0:T(8,128)(2,1)S(1)}, bf16[256,768]{1,0:T(8,128)(2,1)S(1)}, u32[]{:S(2)}, u32[]{:S(2)}) collective-permute-start(bf16[256,768]{1,0:T(8,128)(2,1)S(1)} %constant_dynamic-update-slice_fusion.refs_0_), channel_id=1, source_target_pairs={{0,4},{4,8},{8,12},{12,16},{16,20},{20,24},{24,28},{28,0},{1,5},{5... | collective-permute-start | bytes 1179656 | tf_op jit(solution)/shard_map/ppermute | solution.py:26
  33.2 8.6 %collective-permute-start.5 = (bf16[256,768]{1,0:T(8,128)(2,1)S(1)}, bf16[256,768]{1,0:T(8,128)(2,1)S(1)}, u32[]{:S(2)}, u32[]{:S(2)}) collective-permute-start(bf16[256,768]{1,0:T(8,128)(2,1)S(1)} %collective-permute-done.3.refs_1_), channel_id=1, source_target_pairs={{0,28},{4,0},{8,4},{12,8},{16,12},{20,16},{24,20},{28,24},{1,29},{... | collective-permute-start | bytes 1179656 | tf_op jit(solution)/shard_map/ppermute | solution.py:26
  33.5 9.8 %collective-permute-start.6 = (bf16[256,768]{1,0:T(8,128)(2,1)S(1)}, bf16[256,768]{1,0:T(8,128)(2,1)}, u32[]{:S(2)}, u32[]{:S(2)}) collective-permute-start(bf16[256,768]{1,0:T(8,128)(2,1)S(1)} %collective-permute-done.4.refs_2_), channel_id=1, source_target_pairs={{0,4},{4,8},{8,12},{12,16},{16,20},{20,24},{24,28},{28,0},{1,5},{5... | collective-permute-start | bytes 1179656 | tf_op jit(solution)/shard_map/ppermute | solution.py:26
  41.8 10.9 %copy-start.4 = (bf16[256,768]{1,0:T(8,128)(2,1)}, bf16[256,768]{1,0:T(8,128)(2,1)S(1)}, u32[]{:S(2)}) copy-start(bf16[256,768]{1,0:T(8,128)(2,1)S(1)} %collective-permute-done.5.refs_3_) | copy-start | bytes 1179652
  43.3 7.8 %collective-permute-start.7 = (bf16[256,768]{1,0:T(8,128)(2,1)S(1)}, bf16[256,768]{1,0:T(8,128)(2,1)S(1)}, u32[]{:S(2)}, u32[]{:S(2)}) collective-permute-start(bf16[256,768]{1,0:T(8,128)(2,1)S(1)} %collective-permute-done.5.refs_3_), channel_id=1, source_target_pairs={{0,28},{4,0},{8,4},{12,8},{16,12},{20,16},{24,20},{28,24},{1,29},{... | collective-permute-start | bytes 1179656 | tf_op jit(solution)/shard_map/ppermute | solution.py:26
  43.5 9.2 %collective-permute-start.8 = (bf16[256,768]{1,0:T(8,128)(2,1)}, bf16[256,768]{1,0:T(8,128)(2,1)S(1)}, u32[]{:S(2)}, u32[]{:S(2)}) collective-permute-start(bf16[256,768]{1,0:T(8,128)(2,1)} %collective-permute-done.6.refs_4_), channel_id=1, source_target_pairs={{0,4},{4,8},{8,12},{12,16},{16,20},{20,24},{24,28},{28,0},{1,5},{5... | collective-permute-start | bytes 1179656 | tf_op jit(solution)/shard_map/ppermute | solution.py:26
  48.3 1.3 copy-start.3
  52.7 8.6 %collective-permute-start.11 = (bf16[4,5,32,768]{3,2,1,0:T(8,128)(2,1)S(1)}, bf16[4,5,32,768]{3,2,1,0:T(8,128)(2,1)S(1)}, u32[]{:S(2)}, u32[]{:S(2)}) collective-permute-start(bf16[4,5,32,768]{3,2,1,0:T(8,128)(2,1)S(1)} %get-tuple-element.92), channel_id=1, source_target_pairs={{0,32},{32,0},{1,33},{33,1},{2,34},{34,2},{3,35},{35,3},{4,36},{36... | collective-permute-start | bytes 2949128 | tf_op jit(solution)/shard_map/ppermute | solution.py:26
  52.8 8.5 %collective-permute-start.9 = (bf16[128,768]{1,0:T(8,128)(2,1)S(1)}, bf16[128,768]{1,0:T(8,128)(2,1)S(1)}, u32[]{:S(2)}, u32[]{:S(2)}) collective-permute-start(bf16[128,768]{1,0:T(8,128)(2,1)S(1)} %slice.32), channel_id=1, source_target_pairs={{0,4},{4,8},{8,12},{12,16},{16,20},{20,24},{24,28},{28,0},{1,5},{5... | collective-permute-start | bytes 589832 | tf_op jit(solution)/shard_map/ppermute | solution.py:26
  53.5 7.8 %collective-permute-start.10 = (bf16[128,768]{1,0:T(8,128)(2,1)S(1)}, bf16[128,768]{1,0:T(8,128)(2,1)S(1)}, u32[]{:S(2)}, u32[]{:S(2)}) collective-permute-start(bf16[128,768]{1,0:T(8,128)(2,1)S(1)} %slice.33), channel_id=1, source_target_pairs={{0,28},{4,0},{8,4},{12,8},{16,12},{20,16},{24,20},{28,24},{1,29},{... | collective-permute-start | bytes 589832 | tf_op jit(solution)/shard_map/ppermute | solution.py:26
  63.1 2.3 %collective-permute-start.12 = (bf16[4,3,32,768]{3,2,1,0:T(8,128)(2,1)S(1)}, bf16[4,3,32,768]{3,2,1,0:T(8,128)(2,1)S(1)}, u32[]{:S(2)}, u32[]{:S(2)}) collective-permute-start(bf16[4,3,32,768]{3,2,1,0:T(8,128)(2,1)S(1)} %get-tuple-element.97), channel_id=1, source_target_pairs={{0,32},{32,0},{1,33},{33,1},{2,34},{34,2},{3,35},{35,3},{4,36},{36... | collective-permute-start | bytes 1769480 | tf_op jit(solution)/shard_map/ppermute | solution.py:26
  65.5 8.4 %copy-start.5 = (bf16[256,768]{1,0:T(8,128)(2,1)S(1)}, bf16[256,768]{1,0:T(8,128)(2,1)}, u32[]{:S(2)}) copy-start(bf16[256,768]{1,0:T(8,128)(2,1)} %copy-done.4) | copy-start | bytes 1179652
  68.2 12.7 %collective-permute-start.13 = (bf16[8,32,768]{2,1,0:T(8,128)(2,1)}, bf16[8,32,768]{2,1,0:T(8,128)(2,1)}, u32[]{:S(2)}, u32[]{:S(2)}) collective-permute-start(bf16[8,32,768]{2,1,0:T(8,128)(2,1)} %get-tuple-element.99), channel_id=1, source_target_pairs={{0,64},{64,128},{128,192},{192,0},{1,65},{65,129},{129,193},{193,1... | collective-permute-start | bytes 1179656 | tf_op jit(solution)/shard_map/ppermute | solution.py:26
  69.7 20.7 %collective-permute-start.14 = (bf16[8,32,768]{2,1,0:T(8,128)(2,1)}, bf16[8,32,768]{2,1,0:T(8,128)(2,1)}, u32[]{:S(2)}, u32[]{:S(2)}) collective-permute-start(bf16[8,32,768]{2,1,0:T(8,128)(2,1)} %get-tuple-element.100), channel_id=1, source_target_pairs={{0,128},{64,192},{128,0},{192,64},{1,129},{65,193},{129,1},{193,65... | collective-permute-start | bytes 1179656 | tf_op jit(solution)/shard_map/ppermute | solution.py:26
  72.6 17.9 %collective-permute-start.15 = (bf16[8,32,768]{2,1,0:T(8,128)(2,1)}, bf16[8,32,768]{2,1,0:T(8,128)(2,1)}, u32[]{:S(2)}, u32[]{:S(2)}) collective-permute-start(bf16[8,32,768]{2,1,0:T(8,128)(2,1)} %get-tuple-element.101), channel_id=1, source_target_pairs={{0,192},{64,0},{128,64},{192,128},{1,193},{65,1},{129,65},{193,129... | collective-permute-start | bytes 1179656 | tf_op jit(solution)/shard_map/ppermute | solution.py:26
  73.9 16.6 %copy-start = (bf16[2048,768]{1,0:T(8,128)(2,1)S(1)}, bf16[2048,768]{1,0:T(8,128)(2,1)}, u32[]{:S(2)}) copy-start(bf16[2048,768]{1,0:T(8,128)(2,1)} %all-gather.3.cloned.1.call-done.hid_ref) | copy-start | bytes 9437188
  92.4 17.3 %copy-start.2 = (bf16[768,768]{1,0:T(8,128)(2,1)S(1)}, bf16[768,768]{1,0:T(8,128)(2,1)}, u32[]{:S(2)}) copy-start(bf16[768,768]{1,0:T(8,128)(2,1)} %w_ref.3) | copy-start | bytes 3538948
  92.4 10.8 %collective-permute-start.16 = (bf16[4,32,768]{2,1,0:T(8,128)(2,1)S(1)}, bf16[4,32,768]{2,1,0:T(8,128)(2,1)S(1)}, u32[]{:S(2)}, u32[]{:S(2)}) collective-permute-start(bf16[4,32,768]{2,1,0:T(8,128)(2,1)S(1)} %get-tuple-element.106.refs_0_), channel_id=1, source_target_pairs={{0,192},{64,0},{128,64},{192,128},{1,193},{65,1},{129,65},{193,129... | collective-permute-start | bytes 589832 | tf_op jit(solution)/shard_map/ppermute | solution.py:26
  94.7 9.3 %collective-permute-start.17 = (bf16[4,32,768]{2,1,0:T(8,128)(2,1)S(1)}, bf16[4,32,768]{2,1,0:T(8,128)(2,1)S(1)}, u32[]{:S(2)}, u32[]{:S(2)}) collective-permute-start(bf16[4,32,768]{2,1,0:T(8,128)(2,1)S(1)} %get-tuple-element.106.refs_0_), channel_id=1, source_target_pairs={{0,128},{64,192},{128,0},{192,64},{1,129},{65,193},{129,1},{193,65... | collective-permute-start | bytes 589832 | tf_op jit(solution)/shard_map/ppermute | solution.py:26
  95.8 11.0 %collective-permute-start.18 = (bf16[4,32,768]{2,1,0:T(8,128)(2,1)S(1)}, bf16[4,32,768]{2,1,0:T(8,128)(2,1)S(1)}, u32[]{:S(2)}, u32[]{:S(2)}) collective-permute-start(bf16[4,32,768]{2,1,0:T(8,128)(2,1)S(1)} %get-tuple-element.106.refs_0_), channel_id=1, source_target_pairs={{0,64},{64,128},{128,192},{192,0},{1,65},{65,129},{129,193},{193,1... | collective-permute-start | bytes 589832 | tf_op jit(solution)/shard_map/ppermute | solution.py:26
  107.4 2.4 %collective-permute-start.19 = (bf16[4,4,32,768]{3,2,1,0:T(8,128)(2,1)S(1)}, bf16[4,4,32,768]{3,2,1,0:T(8,128)(2,1)S(1)}, u32[]{:S(2)}, u32[]{:S(2)}) collective-permute-start(bf16[4,4,32,768]{3,2,1,0:T(8,128)(2,1)S(1)} %stack_pre.2.ours_ref), channel_id=1, source_target_pairs={{0,32},{32,0},{1,33},{33,1},{2,34},{34,2},{3,35},{35,3},{4,36},{36... | collective-permute-start | bytes 2359304 | tf_op jit(solution)/shard_map/ppermute | solution.py:26
  112.7 28.8 %collective-permute-start.23 = (bf16[4,64,768]{2,1,0:T(8,128)(2,1)S(1)}, bf16[4,64,768]{2,1,0:T(8,128)(2,1)S(1)}, u32[]{:S(2)}, u32[]{:S(2)}) collective-permute-start(bf16[4,64,768]{2,1,0:T(8,128)(2,1)S(1)} %get-tuple-element.116), channel_id=1, source_target_pairs={{0,1},{1,2},{2,3},{3,0},{4,5},{5,6},{6,7},{7,4},{8,9},{9,10},{10,1... | collective-permute-start | bytes 1179656 | tf_op jit(solution)/shard_map/ppermute | solution.py:26
  114.3 27.2 %collective-permute-start.24 = (bf16[4,64,768]{2,1,0:T(8,128)(2,1)S(1)}, bf16[4,64,768]{2,1,0:T(8,128)(2,1)S(1)}, u32[]{:S(2)}, u32[]{:S(2)}) collective-permute-start(bf16[4,64,768]{2,1,0:T(8,128)(2,1)S(1)} %get-tuple-element.117), channel_id=1, source_target_pairs={{0,3},{1,0},{2,1},{3,2},{4,7},{5,4},{6,5},{7,6},{8,11},{9,8},{10,9... | collective-permute-start | bytes 1179656 | tf_op jit(solution)/shard_map/ppermute | solution.py:26
  119.0 17.5 %collective-permute-start.20 = (bf16[4,32,768]{2,1,0:T(8,128)(2,1)S(1)}, bf16[4,32,768]{2,1,0:T(8,128)(2,1)S(1)}, u32[]{:S(2)}, u32[]{:S(2)}) collective-permute-start(bf16[4,32,768]{2,1,0:T(8,128)(2,1)S(1)} %get-tuple-element.115.refs_0_), channel_id=1, source_target_pairs={{0,192},{64,0},{128,64},{192,128},{1,193},{65,1},{129,65},{193,129... | collective-permute-start | bytes 589832 | tf_op jit(solution)/shard_map/ppermute | solution.py:26
  129.4 9.4 %collective-permute-start.21 = (bf16[4,32,768]{2,1,0:T(8,128)(2,1)S(1)}, bf16[4,32,768]{2,1,0:T(8,128)(2,1)S(1)}, u32[]{:S(2)}, u32[]{:S(2)}) collective-permute-start(bf16[4,32,768]{2,1,0:T(8,128)(2,1)S(1)} %get-tuple-element.115.refs_0_), channel_id=1, source_target_pairs={{0,128},{64,192},{128,0},{192,64},{1,129},{65,193},{129,1},{193,65... | collective-permute-start | bytes 589832 | tf_op jit(solution)/shard_map/ppermute | solution.py:26
  130.1 11.3 %collective-permute-start.22 = (bf16[4,32,768]{2,1,0:T(8,128)(2,1)S(1)}, bf16[4,32,768]{2,1,0:T(8,128)(2,1)S(1)}, u32[]{:S(2)}, u32[]{:S(2)}) collective-permute-start(bf16[4,32,768]{2,1,0:T(8,128)(2,1)S(1)} %get-tuple-element.115.refs_0_), channel_id=1, source_target_pairs={{0,64},{64,128},{128,192},{192,0},{1,65},{65,129},{129,193},{193,1... | collective-permute-start | bytes 589832 | tf_op jit(solution)/shard_map/ppermute | solution.py:26
  142.1 2.4 %collective-permute-start.25 = (bf16[4,4,32,768]{3,2,1,0:T(8,128)(2,1)S(1)}, bf16[4,4,32,768]{3,2,1,0:T(8,128)(2,1)S(1)}, u32[]{:S(2)}, u32[]{:S(2)}) collective-permute-start(bf16[4,4,32,768]{3,2,1,0:T(8,128)(2,1)S(1)} %stack_pre.3.ours_ref), channel_id=1, source_target_pairs={{0,32},{32,0},{1,33},{33,1},{2,34},{34,2},{3,35},{35,3},{4,36},{36... | collective-permute-start | bytes 2359304 | tf_op jit(solution)/shard_map/ppermute | solution.py:26
  142.2 13.0 %collective-permute-start.26 = (bf16[4,64,768]{2,1,0:T(8,128)(2,1)S(1)}, bf16[4,64,768]{2,1,0:T(8,128)(2,1)S(1)}, u32[]{:S(2)}, u32[]{:S(2)}) collective-permute-start(bf16[4,64,768]{2,1,0:T(8,128)(2,1)S(1)} %get-tuple-element.128), channel_id=1, source_target_pairs={{0,2},{1,3},{2,0},{3,1},{4,6},{5,7},{6,4},{7,5},{8,10},{9,11},{10,... | collective-permute-start | bytes 1179656 | tf_op jit(solution)/shard_map/ppermute | solution.py:26
  147.4 20.8 %copy-start.8 = (f32[4,64,768]{2,1,0:T(8,128)}, f32[4,64,768]{2,1,0:T(8,128)S(1)}, u32[]{:S(2)}) copy-start(f32[4,64,768]{2,1,0:T(8,128)S(1)} %get-tuple-element.124) | copy-start | bytes 2359300
  155.2 20.9 %copy-start.6 = (bf16[4,256,768]{2,1,0:T(8,128)(2,1)S(1)}, bf16[4,256,768]{2,1,0:T(8,128)(2,1)}, u32[]{:S(2)}) copy-start(bf16[4,256,768]{2,1,0:T(8,128)(2,1)} %get-tuple-element.148.refs_0_) | copy-start | bytes 4718596
  155.2 20.9 %copy-start.7 = (bf16[4,256,768]{2,1,0:T(8,128)(2,1)S(1)}, bf16[4,256,768]{2,1,0:T(8,128)(2,1)}, u32[]{:S(2)}) copy-start(bf16[4,256,768]{2,1,0:T(8,128)(2,1)} %get-tuple-element.150.refs_1_) | copy-start | bytes 4718596
  155.4 11.9 %collective-permute-start.29 = (bf16[4,64,768]{2,1,0:T(8,128)(2,1)S(1)}, bf16[4,64,768]{2,1,0:T(8,128)(2,1)S(1)}, u32[]{:S(2)}, u32[]{:S(2)}) collective-permute-start(bf16[4,64,768]{2,1,0:T(8,128)(2,1)S(1)} %get-tuple-element.138), channel_id=1, source_target_pairs={{0,1},{1,2},{2,3},{3,0},{4,5},{5,6},{6,7},{7,4},{8,9},{9,10},{10,1... | collective-permute-start | bytes 1179656 | tf_op jit(solution)/shard_map/ppermute | solution.py:26
  156.6 10.7 %collective-permute-start.30 = (bf16[4,64,768]{2,1,0:T(8,128)(2,1)S(1)}, bf16[4,64,768]{2,1,0:T(8,128)(2,1)S(1)}, u32[]{:S(2)}, u32[]{:S(2)}) collective-permute-start(bf16[4,64,768]{2,1,0:T(8,128)(2,1)S(1)} %get-tuple-element.139), channel_id=1, source_target_pairs={{0,3},{1,0},{2,1},{3,2},{4,7},{5,4},{6,5},{7,6},{8,11},{9,8},{10,9... | collective-permute-start | bytes 1179656 | tf_op jit(solution)/shard_map/ppermute | solution.py:26
  158.5 5.8 %collective-permute-start.27 = (bf16[64,768]{1,0:T(8,128)(2,1)S(1)}, bf16[64,768]{1,0:T(8,128)(2,1)S(1)}, u32[]{:S(2)}, u32[]{:S(2)}) collective-permute-start(bf16[64,768]{1,0:T(8,128)(2,1)S(1)} %get-tuple-element.136), channel_id=1, source_target_pairs={{0,4},{4,8},{8,12},{12,16},{16,20},{20,24},{24,28},{28,0},{1,5},{5... | collective-permute-start | bytes 294920 | tf_op jit(solution)/shard_map/ppermute | solution.py:26
  158.5 5.8 %collective-permute-start.28 = (bf16[64,768]{1,0:T(8,128)(2,1)S(1)}, bf16[64,768]{1,0:T(8,128)(2,1)S(1)}, u32[]{:S(2)}, u32[]{:S(2)}) collective-permute-start(bf16[64,768]{1,0:T(8,128)(2,1)S(1)} %get-tuple-element.137), channel_id=1, source_target_pairs={{0,28},{4,0},{8,4},{12,8},{16,12},{20,16},{24,20},{28,24},{1,29},{... | collective-permute-start | bytes 294920 | tf_op jit(solution)/shard_map/ppermute | solution.py:26
  167.4 5.5 %copy-start.10 = (bf16[4,64,768]{2,1,0:T(8,128)(2,1)}, bf16[4,64,768]{2,1,0:T(8,128)(2,1)S(1)}, u32[]{:S(2)}) copy-start(bf16[4,64,768]{2,1,0:T(8,128)(2,1)S(1)} %collective-permute-done.29) | copy-start | bytes 1179652
  167.4 5.5 %copy-start.12 = (bf16[4,64,768]{2,1,0:T(8,128)(2,1)}, bf16[4,64,768]{2,1,0:T(8,128)(2,1)S(1)}, u32[]{:S(2)}) copy-start(bf16[4,64,768]{2,1,0:T(8,128)(2,1)S(1)} %collective-permute-done.30) | copy-start | bytes 1179652
  168.2 14.1 %collective-permute-start.33 = (bf16[4,64,768]{2,1,0:T(8,128)(2,1)S(1)}, bf16[4,64,768]{2,1,0:T(8,128)(2,1)}, u32[]{:S(2)}, u32[]{:S(2)}) collective-permute-start(bf16[4,64,768]{2,1,0:T(8,128)(2,1)S(1)} %get-tuple-element.146), channel_id=1, source_target_pairs={{0,2},{1,3},{2,0},{3,1},{4,6},{5,7},{6,4},{7,5},{8,10},{9,11},{10,... | collective-permute-start | bytes 1179656 | tf_op jit(solution)/shard_map/ppermute | solution.py:26
  172.9 9.4 %collective-permute-start.31 = (bf16[64,768]{1,0:T(8,128)(2,1)}, bf16[64,768]{1,0:T(8,128)(2,1)}, u32[]{:S(2)}, u32[]{:S(2)}) collective-permute-start(bf16[64,768]{1,0:T(8,128)(2,1)} %get-tuple-element.144), channel_id=1, source_target_pairs={{0,4},{4,8},{8,12},{12,16},{16,20},{20,24},{24,28},{28,0},{1,5},{5... | collective-permute-start | bytes 294920 | tf_op jit(solution)/shard_map/ppermute | solution.py:26
  172.9 9.4 %collective-permute-start.32 = (bf16[64,768]{1,0:T(8,128)(2,1)}, bf16[64,768]{1,0:T(8,128)(2,1)}, u32[]{:S(2)}, u32[]{:S(2)}) collective-permute-start(bf16[64,768]{1,0:T(8,128)(2,1)} %get-tuple-element.145), channel_id=1, source_target_pairs={{0,28},{4,0},{8,4},{12,8},{16,12},{20,16},{24,20},{28,24},{1,29},{... | collective-permute-start | bytes 294920 | tf_op jit(solution)/shard_map/ppermute | solution.py:26
  176.1 6.1 %copy-start.9 = (f32[4,64,768]{2,1,0:T(8,128)S(1)}, f32[4,64,768]{2,1,0:T(8,128)}, u32[]{:S(2)}) copy-start(f32[4,64,768]{2,1,0:T(8,128)} %copy-done.8) | copy-start | bytes 2359300
  176.2 6.1 %copy-start.11 = (bf16[4,64,768]{2,1,0:T(8,128)(2,1)S(1)}, bf16[4,64,768]{2,1,0:T(8,128)(2,1)}, u32[]{:S(2)}) copy-start(bf16[4,64,768]{2,1,0:T(8,128)(2,1)} %copy-done.10) | copy-start | bytes 1179652
  176.2 6.1 %copy-start.13 = (bf16[4,64,768]{2,1,0:T(8,128)(2,1)S(1)}, bf16[4,64,768]{2,1,0:T(8,128)(2,1)}, u32[]{:S(2)}) copy-start(bf16[4,64,768]{2,1,0:T(8,128)(2,1)} %copy-done.12) | copy-start | bytes 1179652
  184.5 5.9 %collective-permute-start.34 = (bf16[64,768]{1,0:T(8,128)(2,1)S(1)}, bf16[64,768]{1,0:T(8,128)(2,1)S(1)}, u32[]{:S(2)}, u32[]{:S(2)}) collective-permute-start(bf16[64,768]{1,0:T(8,128)(2,1)S(1)} %get-tuple-element.155), channel_id=1, source_target_pairs={{0,4},{4,8},{8,12},{12,16},{16,20},{20,24},{24,28},{28,0},{1,5},{5... | collective-permute-start | bytes 294920 | tf_op jit(solution)/shard_map/ppermute | solution.py:26
  184.6 5.8 %collective-permute-start.35 = (bf16[64,768]{1,0:T(8,128)(2,1)S(1)}, bf16[64,768]{1,0:T(8,128)(2,1)S(1)}, u32[]{:S(2)}, u32[]{:S(2)}) collective-permute-start(bf16[64,768]{1,0:T(8,128)(2,1)S(1)} %get-tuple-element.156), channel_id=1, source_target_pairs={{0,28},{4,0},{8,4},{12,8},{16,12},{20,16},{24,20},{28,24},{1,29},{... | collective-permute-start | bytes 294920 | tf_op jit(solution)/shard_map/ppermute | solution.py:26
  190.4 5.9 %collective-permute-start.36 = (bf16[64,768]{1,0:T(8,128)(2,1)S(1)}, bf16[64,768]{1,0:T(8,128)(2,1)S(1)}, u32[]{:S(2)}, u32[]{:S(2)}) collective-permute-start(bf16[64,768]{1,0:T(8,128)(2,1)S(1)} %fusion.1), channel_id=1, source_target_pairs={{0,4},{4,8},{8,12},{12,16},{16,20},{20,24},{24,28},{28,0},{1,5},{5... | collective-permute-start | bytes 294920 | tf_op jit(solution)/shard_map/ppermute | solution.py:26
Sparse Core Ops, SparseCore 0:
  9.8 33.1 all-gather.2
  45.6 78.7 all-gather.4

commit v2 on v1

--- a/solution.py
+++ b/solution.py
@@ -18,7 +18,7 @@
 ORDER = tuple(s for group in GROUPS for s in group)
 BACK = ((4, -3, 3, -2), (2, -1, 1, 0))
 FEATURES = 768
-LIMIT = 48 * 1024 * 1024
+LIMIT = 20 * 1024 * 1024
 
 
 def shift(a, axis, by):

time: 208 us -> 207 us (level)
  Pallas kernels: 29.5 us -> 24.2 us
  local copies, waits for them, and re-layouts: 2.35 us -> 4.86 us
    pallas_call x10, Pallas kernels: 29.5 us -> 24.2 us  [call(): pl.pallas_call(body, in_specs=[pl.BlockSpec(memory_space=pltpu.SMEM)] + [...]
    unnamed x32 -> x30, local copies, waits for them, and re-layouts: 2.28 us -> 4.79 us
  transfers between devices with their start and end apart: 39 -> 39, of which waited for: 24 -> 24; matrix products, arithmetic and copies ran while one was open for 1% -> 1% of each run, Pallas kernels for 14% -> 12%
where the time goes in v2:
time: 207 us; the launch traced here: 203 us
  waiting for transfers between devices  88.2 us (43%)
  starting transfers between devices  67 us (32%)
  Pallas kernels  24.2 us (12%)
  between operations  14.5 us (7%)
  local copies, waits for them, and re-layouts  4.86 us (2%)
  other arithmetic  3.9 us (2%)
    ppermute x37, waiting for transfers between devices, shift(): return lax.ppermute(a, axis, [(i, (i + by) % n) for i in range(n)])  87.5 us
    ppermute x37, starting transfers between devices, shift(): return lax.ppermute(a, axis, [(i, (i + by) % n) for i in range(n)])  66.9 us
    pallas_call x10, Pallas kernels, call(): pl.pallas_call(body, in_specs=[pl.BlockSpec(memory_space=pltpu.SMEM)] + [...  24.2 us
    unnamed x30, local copies, waits for them, and re-layouts  4.79 us
  transfers between devices with their start and end apart: 39, of which 24 were waited for; matrix products, arithmetic and copies ran while one was open for 1% of the time, Pallas kernels for 12%

profile of v2, /device:TPU:8, one launch (start us, length us, event | category | flops | bytes accessed | tf_op | source)
XLA Modules:
  0.0 202.6 jit_solution(18138024251783811324)
XLA Ops:
  7.2 0.7 all-gather.3.cloned.1.call-update
  8.0 2.3 %collective-permute-start = (bf16[64,768]{1,0:T(8,128)(2,1)}, bf16[64,768]{1,0:T(8,128)(2,1)S(1)}, u32[]{:S(2)}, u32[]{:S(2)}) collective-permute-start(bf16[64,768]{1,0:T(8,128)(2,1)} %param.6), channel_id=1, source_target_pairs={{0,3},{1,0},{2,1},{3,2},{4,7},{5,4},{6,5},{7,6},{8,11},{9,8},{10,9... | collective-permute-start | bytes 294920 | tf_op jit(solution)/shard_map/ppermute | solution.py:26
  10.2 0.9 collective-permute-start.1
  11.1 1.9 collective-permute-start.2
  13.0 0.9 constant_dynamic-update-slice_fusion.3
  13.9 2.6 %collective-permute-done.1 = bf16[64,768]{1,0:T(8,128)(2,1)S(1)} collective-permute-done((bf16[64,768]{1,0:T(8,128)(2,1)}, bf16[64,768]{1,0:T(8,128)(2,1)S(1)}, u32[]{:S(2)}, u32[]{:S(2)}) %collective-permute-start.1) | collective-permute-done | bytes 98336 | tf_op jit(solution)/shard_map/ppermute | solution.py:26
  16.7 5.9 %collective-permute-start.3 = (bf16[256,768]{1,0:T(8,128)(2,1)S(1)}, bf16[256,768]{1,0:T(8,128)(2,1)S(1)}, u32[]{:S(2)}, u32[]{:S(2)}) collective-permute-start(bf16[256,768]{1,0:T(8,128)(2,1)S(1)} %constant_dynamic-update-slice_fusion.refs_0_), channel_id=1, source_target_pairs={{0,28},{4,0},{8,4},{12,8},{16,12},{20,16},{24,20},{28,24},{1,29},{... | collective-permute-start | bytes 1179656 | tf_op jit(solution)/shard_map/ppermute | solution.py:26
  22.6 7.2 %collective-permute-done.3.refs_1_ = bf16[256,768]{1,0:T(8,128)(2,1)S(1)} collective-permute-done((bf16[256,768]{1,0:T(8,128)(2,1)S(1)}, bf16[256,768]{1,0:T(8,128)(2,1)S(1)}, u32[]{:S(2)}, u32[]{:S(2)}) %collective-permute-start.3) | collective-permute-done | bytes 393248 | tf_op jit(solution)/shard_map/ppermute | solution.py:26
  29.8 3.4 %collective-permute-done.4.refs_2_ = bf16[256,768]{1,0:T(8,128)(2,1)S(1)} collective-permute-done((bf16[256,768]{1,0:T(8,128)(2,1)S(1)}, bf16[256,768]{1,0:T(8,128)(2,1)S(1)}, u32[]{:S(2)}, u32[]{:S(2)}) %collective-permute-start.4) | collective-permute-done | bytes 393248 | tf_op jit(solution)/shard_map/ppermute | solution.py:26
  33.5 1.7 collective-permute-start.6
  35.2 6.5 %collective-permute-done.5.refs_3_ = bf16[256,768]{1,0:T(8,128)(2,1)S(1)} collective-permute-done((bf16[256,768]{1,0:T(8,128)(2,1)S(1)}, bf16[256,768]{1,0:T(8,128)(2,1)S(1)}, u32[]{:S(2)}, u32[]{:S(2)}) %collective-permute-start.5) | collective-permute-done | bytes 393248 | tf_op jit(solution)/shard_map/ppermute | solution.py:26
  41.8 1.5 collective-permute-done.6.refs_4_
  43.5 1.8 collective-permute-start.8
  45.4 2.9 %act_products.2 = (f32[4,5,32,768]{3,2,1,0:T(8,128)S(1)}, bf16[4,5,32,768]{3,2,1,0:T(8,128)(2,1)S(1)}) custom-call(s32[4]{0:T(128)S(1)} %pad_add_fusion.pos, bf16[256,768]{1,0:T(8,128)(2,1)S(1)} %constant_dynamic-update-slice_fusion.refs_0_, bf16[256,768]{1,0:T(8,128)(2,1)S(1)} %collective-permute-done.3.refs_1_, ...), custom_call_target="tpu_custom_call" | custom-call | flops 1 | bytes 1 | tf_op jit(solution)/shard_map/act_products/pallas_call | solution.py:38
  48.3 2.8 %collective-permute-done.7.refs_0_.refs_5_ = bf16[256,768]{1,0:T(8,128)(2,1)S(1)} collective-permute-done((bf16[256,768]{1,0:T(8,128)(2,1)S(1)}, bf16[256,768]{1,0:T(8,128)(2,1)S(1)}, u32[]{:S(2)}, u32[]{:S(2)}) %collective-permute-start.7) | collective-permute-done | bytes 393248 | tf_op jit(solution)/shard_map/ppermute | solution.py:26
  51.1 1.6 collective-permute-done.8.refs_1_.refs_6_
  52.8 0.7 collective-permute-start.9
  53.5 2.6 %collective-permute-start.10 = (bf16[128,768]{1,0:T(8,128)(2,1)S(1)}, bf16[128,768]{1,0:T(8,128)(2,1)S(1)}, u32[]{:S(2)}, u32[]{:S(2)}) collective-permute-start(bf16[128,768]{1,0:T(8,128)(2,1)S(1)} %slice.33), channel_id=1, source_target_pairs={{0,28},{4,0},{8,4},{12,8},{16,12},{20,16},{24,20},{28,24},{1,29},{... | collective-permute-start | bytes 589832 | tf_op jit(solution)/shard_map/ppermute | solution.py:26
  56.1 5.2 %collective-permute-done.9 = bf16[128,768]{1,0:T(8,128)(2,1)S(1)} collective-permute-done((bf16[128,768]{1,0:T(8,128)(2,1)S(1)}, bf16[128,768]{1,0:T(8,128)(2,1)S(1)}, u32[]{:S(2)}, u32[]{:S(2)}) %collective-permute-start.9) | collective-permute-done | bytes 196640 | tf_op jit(solution)/shard_map/ppermute | solution.py:26
  61.4 1.7 act_products.3
  63.5 2.0 collective-permute-done.12.refs_3_
  65.5 1.7 fold.1
  67.2 1.5 collective-permute-start.13
  68.7 2.8 %collective-permute-start.14 = (bf16[8,32,768]{2,1,0:T(8,128)(2,1)}, bf16[8,32,768]{2,1,0:T(8,128)(2,1)}, u32[]{:S(2)}, u32[]{:S(2)}) collective-permute-start(bf16[8,32,768]{2,1,0:T(8,128)(2,1)} %get-tuple-element.100), channel_id=1, source_target_pairs={{0,128},{64,192},{128,0},{192,64},{1,129},{65,193},{129,1},{193,65... | collective-permute-start | bytes 1179656 | tf_op jit(solution)/shard_map/ppermute | solution.py:26
  71.5 1.3 collective-permute-start.15
  72.9 1.9 copy-done
  74.8 6.2 %grad_w_out.1 = f32[768,768]{1,0:T(8,128)} custom-call(s32[4]{0:T(128)S(1)} %pad_add_fusion.pos, bf16[2048,768]{1,0:T(8,128)(2,1)S(1)} %copy-done, bf16[256,768]{1,0:T(8,128)(2,1)S(1)} %constant_dynamic-update-slice_fusion.refs_0_, bf16[256,768]{1,0:T(8,128)(2,1)S(1)} %collective-permute-done.3.refs_1_, bf16[256,768]{1,0:T(8,128)(2,1)S(1)} %collective-permute-done.4.refs_2_, ...), custom_call_target="tpu_custom_call" | custom-call | flops 1 | bytes 1 | tf_op jit(solution)/shard_map/grad_w_out/pallas_call | solution.py:38
  80.9 8.5 %collective-permute-done.14.t2 = bf16[8,32,768]{2,1,0:T(8,128)(2,1)} collective-permute-done((bf16[8,32,768]{2,1,0:T(8,128)(2,1)}, bf16[8,32,768]{2,1,0:T(8,128)(2,1)}, u32[]{:S(2)}, u32[]{:S(2)}) %collective-permute-start.14) | collective-permute-done | bytes 393248 | tf_op jit(solution)/shard_map/ppermute | solution.py:26
  89.4 1.9 pre_grad.1
  91.3 2.2 %collective-permute-start.16 = (bf16[4,32,768]{2,1,0:T(8,128)(2,1)S(1)}, bf16[4,32,768]{2,1,0:T(8,128)(2,1)S(1)}, u32[]{:S(2)}, u32[]{:S(2)}) collective-permute-start(bf16[4,32,768]{2,1,0:T(8,128)(2,1)S(1)} %get-tuple-element.106.refs_0_), channel_id=1, source_target_pairs={{0,192},{64,0},{128,64},{192,128},{1,193},{65,1},{129,65},{193,129... | collective-permute-start | bytes 589832 | tf_op jit(solution)/shard_map/ppermute | solution.py:26
  93.6 1.1 collective-permute-start.17
  94.7 0.7 collective-permute-start.18
  95.4 6.7 %collective-permute-done.16.refs_1_ = bf16[4,32,768]{2,1,0:T(8,128)(2,1)S(1)} collective-permute-done((bf16[4,32,768]{2,1,0:T(8,128)(2,1)S(1)}, bf16[4,32,768]{2,1,0:T(8,128)(2,1)S(1)}, u32[]{:S(2)}, u32[]{:S(2)}) %collective-permute-start.16) | collective-permute-done | bytes 196640 | tf_op jit(solution)/shard_map/ppermute | solution.py:26
  102.1 0.8 collective-permute-done.17.refs_2_
  102.9 2.8 %collective-permute-done.18.refs_3_ = bf16[4,32,768]{2,1,0:T(8,128)(2,1)S(1)} collective-permute-done((bf16[4,32,768]{2,1,0:T(8,128)(2,1)S(1)}, bf16[4,32,768]{2,1,0:T(8,128)(2,1)S(1)}, u32[]{:S(2)}, u32[]{:S(2)}) %collective-permute-start.18) | collective-permute-done | bytes 196640 | tf_op jit(solution)/shard_map/ppermute | solution.py:26
  106.4 2.3 %collective-permute-done.19.other_ref = bf16[4,4,32,768]{3,2,1,0:T(8,128)(2,1)S(1)} collective-permute-done((bf16[4,4,32,768]{3,2,1,0:T(8,128)(2,1)S(1)}, bf16[4,4,32,768]{3,2,1,0:T(8,128)(2,1)S(1)}, u32[]{:S(2)}, u32[]{:S(2)}) %collective-permute-start.19) | collective-permute-done | bytes 786464 | tf_op jit(solution)/shard_map/ppermute | solution.py:26
  108.7 2.0 grad_x_products.2
  110.6 1.6 collective-permute-start.23
  112.3 5.0 %collective-permute-start.24 = (bf16[4,64,768]{2,1,0:T(8,128)(2,1)S(1)}, bf16[4,64,768]{2,1,0:T(8,128)(2,1)S(1)}, u32[]{:S(2)}, u32[]{:S(2)}) collective-permute-start(bf16[4,64,768]{2,1,0:T(8,128)(2,1)S(1)} %get-tuple-element.117), channel_id=1, source_target_pairs={{0,3},{1,0},{2,1},{3,2},{4,7},{5,4},{6,5},{7,6},{8,11},{9,8},{10,9... | collective-permute-start | bytes 1179656 | tf_op jit(solution)/shard_map/ppermute | solution.py:26
  117.3 10.3 %collective-permute-start.20 = (bf16[4,32,768]{2,1,0:T(8,128)(2,1)S(1)}, bf16[4,32,768]{2,1,0:T(8,128)(2,1)S(1)}, u32[]{:S(2)}, u32[]{:S(2)}) collective-permute-start(bf16[4,32,768]{2,1,0:T(8,128)(2,1)S(1)} %get-tuple-element.115.refs_0_), channel_id=1, source_target_pairs={{0,192},{64,0},{128,64},{192,128},{1,193},{65,1},{129,65},{193,129... | collective-permute-start | bytes 589832 | tf_op jit(solution)/shard_map/ppermute | solution.py:26
  127.6 0.7 collective-permute-start.21
  128.3 0.8 collective-permute-start.22
  129.2 5.6 %collective-permute-done.20.refs_1_ = bf16[4,32,768]{2,1,0:T(8,128)(2,1)S(1)} collective-permute-done((bf16[4,32,768]{2,1,0:T(8,128)(2,1)S(1)}, bf16[4,32,768]{2,1,0:T(8,128)(2,1)S(1)}, u32[]{:S(2)}, u32[]{:S(2)}) %collective-permute-start.20) | collective-permute-done | bytes 196640 | tf_op jit(solution)/shard_map/ppermute | solution.py:26
  134.8 2.2 %collective-permute-done.21.refs_2_ = bf16[4,32,768]{2,1,0:T(8,128)(2,1)S(1)} collective-permute-done((bf16[4,32,768]{2,1,0:T(8,128)(2,1)S(1)}, bf16[4,32,768]{2,1,0:T(8,128)(2,1)S(1)}, u32[]{:S(2)}, u32[]{:S(2)}) %collective-permute-start.21) | collective-permute-done | bytes 196640 | tf_op jit(solution)/shard_map/ppermute | solution.py:26
  137.0 2.7 %collective-permute-done.22.refs_3_ = bf16[4,32,768]{2,1,0:T(8,128)(2,1)S(1)} collective-permute-done((bf16[4,32,768]{2,1,0:T(8,128)(2,1)S(1)}, bf16[4,32,768]{2,1,0:T(8,128)(2,1)S(1)}, u32[]{:S(2)}, u32[]{:S(2)}) %collective-permute-start.22) | collective-permute-done | bytes 196640 | tf_op jit(solution)/shard_map/ppermute | solution.py:26
  140.4 2.1 %collective-permute-start.26 = (bf16[4,64,768]{2,1,0:T(8,128)(2,1)S(1)}, bf16[4,64,768]{2,1,0:T(8,128)(2,1)S(1)}, u32[]{:S(2)}, u32[]{:S(2)}) collective-permute-start(bf16[4,64,768]{2,1,0:T(8,128)(2,1)S(1)} %get-tuple-element.128), channel_id=1, source_target_pairs={{0,2},{1,3},{2,0},{3,1},{4,6},{5,7},{6,4},{7,5},{8,10},{9,11},{10,... | collective-permute-start | bytes 1179656 | tf_op jit(solution)/shard_map/ppermute | solution.py:26
  142.7 2.0 grad_x_products.3
  144.7 8.8 %collective-permute-done.26 = bf16[4,64,768]{2,1,0:T(8,128)(2,1)S(1)} collective-permute-done((bf16[4,64,768]{2,1,0:T(8,128)(2,1)S(1)}, bf16[4,64,768]{2,1,0:T(8,128)(2,1)S(1)}, u32[]{:S(2)}, u32[]{:S(2)}) %collective-permute-start.26) | collective-permute-done | bytes 393248 | tf_op jit(solution)/shard_map/ppermute | solution.py:26
  153.7 1.1 collective-permute-start.29
  154.8 1.9 collective-permute-start.30
  156.7 3.2 %collective-permute-start.28 = (bf16[64,768]{1,0:T(8,128)(2,1)S(1)}, bf16[64,768]{1,0:T(8,128)(2,1)S(1)}, u32[]{:S(2)}, u32[]{:S(2)}) collective-permute-start(bf16[64,768]{1,0:T(8,128)(2,1)S(1)} %get-tuple-element.137), channel_id=1, source_target_pairs={{0,28},{4,0},{8,4},{12,8},{16,12},{20,16},{24,20},{28,24},{1,29},{... | collective-permute-start | bytes 294920 | tf_op jit(solution)/shard_map/ppermute | solution.py:26
  159.9 2.6 %collective-permute-done.27 = bf16[64,768]{1,0:T(8,128)(2,1)S(1)} collective-permute-done((bf16[64,768]{1,0:T(8,128)(2,1)S(1)}, bf16[64,768]{1,0:T(8,128)(2,1)S(1)}, u32[]{:S(2)}, u32[]{:S(2)}) %collective-permute-start.27) | collective-permute-done | bytes 98336 | tf_op jit(solution)/shard_map/ppermute | solution.py:26
  162.5 3.0 %collective-permute-done.29 = bf16[4,64,768]{2,1,0:T(8,128)(2,1)S(1)} collective-permute-done((bf16[4,64,768]{2,1,0:T(8,128)(2,1)S(1)}, bf16[4,64,768]{2,1,0:T(8,128)(2,1)S(1)}, u32[]{:S(2)}, u32[]{:S(2)}) %collective-permute-start.29) | collective-permute-done | bytes 393248 | tf_op jit(solution)/shard_map/ppermute | solution.py:26
  165.5 0.8 fusion.10
  166.3 4.7 %collective-permute-start.33 = (bf16[4,64,768]{2,1,0:T(8,128)(2,1)S(1)}, bf16[4,64,768]{2,1,0:T(8,128)(2,1)}, u32[]{:S(2)}, u32[]{:S(2)}) collective-permute-start(bf16[4,64,768]{2,1,0:T(8,128)(2,1)S(1)} %get-tuple-element.146), channel_id=1, source_target_pairs={{0,2},{1,3},{2,0},{3,1},{4,6},{5,7},{6,4},{7,5},{8,10},{9,11},{10,... | collective-permute-start | bytes 1179656 | tf_op jit(solution)/shard_map/ppermute | solution.py:26
  171.1 3.2 %collective-permute-start.32 = (bf16[64,768]{1,0:T(8,128)(2,1)}, bf16[64,768]{1,0:T(8,128)(2,1)}, u32[]{:S(2)}, u32[]{:S(2)}) collective-permute-start(bf16[64,768]{1,0:T(8,128)(2,1)} %get-tuple-element.145), channel_id=1, source_target_pairs={{0,28},{4,0},{8,4},{12,8},{16,12},{20,16},{24,20},{28,24},{1,29},{... | collective-permute-start | bytes 294920 | tf_op jit(solution)/shard_map/ppermute | solution.py:26
  174.3 1.9 copy-done.4
  176.2 4.7 %grad_w_in.1 = f32[768,768]{1,0:T(8,128)} custom-call(s32[4]{0:T(128)S(1)} %pad_add_fusion.pos, bf16[2048,768]{1,0:T(8,128)(2,1)S(1)} %copy-done.4, bf16[4,256,768]{2,1,0:T(8,128)(2,1)S(1)} %get-tuple-element.148.refs_0_, bf16[4,256,768]{2,1,0:T(8,128)(2,1)S(1)} %get-tuple-element.150.refs_1_), custom_call_target="tpu_custom_call" | custom-call | flops 1 | bytes 1 | tf_op jit(solution)/shard_map/grad_w_in/pallas_call | solution.py:38
  180.9 1.2 convert_add_fusion
  182.1 1.0 fusion.3
  183.1 3.2 %collective-permute-start.35 = (bf16[64,768]{1,0:T(8,128)(2,1)S(1)}, bf16[64,768]{1,0:T(8,128)(2,1)S(1)}, u32[]{:S(2)}, u32[]{:S(2)}) collective-permute-start(bf16[64,768]{1,0:T(8,128)(2,1)S(1)} %get-tuple-element.156), channel_id=1, source_target_pairs={{0,28},{4,0},{8,4},{12,8},{16,12},{20,16},{24,20},{28,24},{1,29},{... | collective-permute-start | bytes 294920 | tf_op jit(solution)/shard_map/ppermute | solution.py:26
  186.4 2.6 %collective-permute-done.34 = bf16[64,768]{1,0:T(8,128)(2,1)S(1)} collective-permute-done((bf16[64,768]{1,0:T(8,128)(2,1)S(1)}, bf16[64,768]{1,0:T(8,128)(2,1)S(1)}, u32[]{:S(2)}, u32[]{:S(2)}) %collective-permute-start.34) | collective-permute-done | bytes 98336 | tf_op jit(solution)/shard_map/ppermute | solution.py:26
  189.1 5.8 %collective-permute-done.36 = bf16[64,768]{1,0:T(8,128)(2,1)S(1)} collective-permute-done((bf16[64,768]{1,0:T(8,128)(2,1)S(1)}, bf16[64,768]{1,0:T(8,128)(2,1)S(1)}, u32[]{:S(2)}, u32[]{:S(2)}) %collective-permute-start.36) | collective-permute-done | bytes 98336 | tf_op jit(solution)/shard_map/ppermute | solution.py:26
  194.9 0.7 fusion.8
  (68 shorter events, 3.3 us)
Async XLA Ops:
  7.2 38.2 %copy-start.2 = (bf16[768,768]{1,0:T(8,128)(2,1)S(1)}, bf16[768,768]{1,0:T(8,128)(2,1)}, u32[]{:S(2)}) copy-start(bf16[768,768]{1,0:T(8,128)(2,1)} %refs_3_.1) | copy-start | bytes 3538948
  7.2 65.7 %all-gather.3.cloned.1.call-start = ((), (), s32[]{:S(2)}) async-start(), calls=%async_computation | async-start | bytes 3538944 | tf_op jit(solution)/shard_map/all_gather | solution.py:159
  7.9 166.4 %all-gather.5.cloned.1.call-start = ((), (), s32[]{:S(2)}) async-start(), calls=%async_computation.1 | async-start | bytes 3244032 | tf_op jit(solution)/shard_map/all_gather | solution.py:202
  8.0 5.9 %collective-permute-start = (bf16[64,768]{1,0:T(8,128)(2,1)}, bf16[64,768]{1,0:T(8,128)(2,1)S(1)}, u32[]{:S(2)}, u32[]{:S(2)}) collective-permute-start(bf16[64,768]{1,0:T(8,128)(2,1)} %param.6), channel_id=1, source_target_pairs={{0,3},{1,0},{2,1},{3,2},{4,7},{5,4},{6,5},{7,6},{8,11},{9,8},{10,9... | collective-permute-start | bytes 294920 | tf_op jit(solution)/shard_map/ppermute | solution.py:26
  10.2 6.3 %collective-permute-start.1 = (bf16[64,768]{1,0:T(8,128)(2,1)}, bf16[64,768]{1,0:T(8,128)(2,1)S(1)}, u32[]{:S(2)}, u32[]{:S(2)}) collective-permute-start(bf16[64,768]{1,0:T(8,128)(2,1)} %param.6), channel_id=1, source_target_pairs={{0,2},{1,3},{2,0},{3,1},{4,6},{5,7},{6,4},{7,5},{8,10},{9,11},{10,... | collective-permute-start | bytes 294920 | tf_op jit(solution)/shard_map/ppermute | solution.py:26
  11.1 5.6 %collective-permute-start.2 = (bf16[64,768]{1,0:T(8,128)(2,1)}, bf16[64,768]{1,0:T(8,128)(2,1)S(1)}, u32[]{:S(2)}, u32[]{:S(2)}) collective-permute-start(bf16[64,768]{1,0:T(8,128)(2,1)} %param.6), channel_id=1, source_target_pairs={{0,1},{1,2},{2,3},{3,0},{4,5},{5,6},{6,7},{7,4},{8,9},{9,10},{10,1... | collective-permute-start | bytes 294920 | tf_op jit(solution)/shard_map/ppermute | solution.py:26
  16.7 13.1 %collective-permute-start.3 = (bf16[256,768]{1,0:T(8,128)(2,1)S(1)}, bf16[256,768]{1,0:T(8,128)(2,1)S(1)}, u32[]{:S(2)}, u32[]{:S(2)}) collective-permute-start(bf16[256,768]{1,0:T(8,128)(2,1)S(1)} %constant_dynamic-update-slice_fusion.refs_0_), channel_id=1, source_target_pairs={{0,28},{4,0},{8,4},{12,8},{16,12},{20,16},{24,20},{28,24},{1,29},{... | collective-permute-start | bytes 1179656 | tf_op jit(solution)/shard_map/ppermute | solution.py:26
  22.6 10.6 %collective-permute-start.4 = (bf16[256,768]{1,0:T(8,128)(2,1)S(1)}, bf16[256,768]{1,0:T(8,128)(2,1)S(1)}, u32[]{:S(2)}, u32[]{:S(2)}) collective-permute-start(bf16[256,768]{1,0:T(8,128)(2,1)S(1)} %constant_dynamic-update-slice_fusion.refs_0_), channel_id=1, source_target_pairs={{0,4},{4,8},{8,12},{12,16},{16,20},{20,24},{24,28},{28,0},{1,5},{5... | collective-permute-start | bytes 1179656 | tf_op jit(solution)/shard_map/ppermute | solution.py:26
  33.2 8.6 %collective-permute-start.5 = (bf16[256,768]{1,0:T(8,128)(2,1)S(1)}, bf16[256,768]{1,0:T(8,128)(2,1)S(1)}, u32[]{:S(2)}, u32[]{:S(2)}) collective-permute-start(bf16[256,768]{1,0:T(8,128)(2,1)S(1)} %collective-permute-done.3.refs_1_), channel_id=1, source_target_pairs={{0,28},{4,0},{8,4},{12,8},{16,12},{20,16},{24,20},{28,24},{1,29},{... | collective-permute-start | bytes 1179656 | tf_op jit(solution)/shard_map/ppermute | solution.py:26
  33.5 9.8 %collective-permute-start.6 = (bf16[256,768]{1,0:T(8,128)(2,1)S(1)}, bf16[256,768]{1,0:T(8,128)(2,1)}, u32[]{:S(2)}, u32[]{:S(2)}) collective-permute-start(bf16[256,768]{1,0:T(8,128)(2,1)S(1)} %collective-permute-done.4.refs_2_), channel_id=1, source_target_pairs={{0,4},{4,8},{8,12},{12,16},{16,20},{20,24},{24,28},{28,0},{1,5},{5... | collective-permute-start | bytes 1179656 | tf_op jit(solution)/shard_map/ppermute | solution.py:26
  41.8 10.9 %copy-start.5 = (bf16[256,768]{1,0:T(8,128)(2,1)}, bf16[256,768]{1,0:T(8,128)(2,1)S(1)}, u32[]{:S(2)}) copy-start(bf16[256,768]{1,0:T(8,128)(2,1)S(1)} %collective-permute-done.5.refs_3_) | copy-start | bytes 1179652
  43.3 7.8 %collective-permute-start.7 = (bf16[256,768]{1,0:T(8,128)(2,1)S(1)}, bf16[256,768]{1,0:T(8,128)(2,1)S(1)}, u32[]{:S(2)}, u32[]{:S(2)}) collective-permute-start(bf16[256,768]{1,0:T(8,128)(2,1)S(1)} %collective-permute-done.5.refs_3_), channel_id=1, source_target_pairs={{0,28},{4,0},{8,4},{12,8},{16,12},{20,16},{24,20},{28,24},{1,29},{... | collective-permute-start | bytes 1179656 | tf_op jit(solution)/shard_map/ppermute | solution.py:26
  43.5 9.2 %collective-permute-start.8 = (bf16[256,768]{1,0:T(8,128)(2,1)}, bf16[256,768]{1,0:T(8,128)(2,1)S(1)}, u32[]{:S(2)}, u32[]{:S(2)}) collective-permute-start(bf16[256,768]{1,0:T(8,128)(2,1)} %collective-permute-done.6.refs_4_), channel_id=1, source_target_pairs={{0,4},{4,8},{8,12},{12,16},{16,20},{20,24},{24,28},{28,0},{1,5},{5... | collective-permute-start | bytes 1179656 | tf_op jit(solution)/shard_map/ppermute | solution.py:26
  52.7 8.6 %collective-permute-start.11 = (bf16[4,5,32,768]{3,2,1,0:T(8,128)(2,1)S(1)}, bf16[4,5,32,768]{3,2,1,0:T(8,128)(2,1)S(1)}, u32[]{:S(2)}, u32[]{:S(2)}) collective-permute-start(bf16[4,5,32,768]{3,2,1,0:T(8,128)(2,1)S(1)} %get-tuple-element.92), channel_id=1, source_target_pairs={{0,32},{32,0},{1,33},{33,1},{2,34},{34,2},{3,35},{35,3},{4,36},{36... | collective-permute-start | bytes 2949128 | tf_op jit(solution)/shard_map/ppermute | solution.py:26
  52.8 8.5 %collective-permute-start.9 = (bf16[128,768]{1,0:T(8,128)(2,1)S(1)}, bf16[128,768]{1,0:T(8,128)(2,1)S(1)}, u32[]{:S(2)}, u32[]{:S(2)}) collective-permute-start(bf16[128,768]{1,0:T(8,128)(2,1)S(1)} %slice.32), channel_id=1, source_target_pairs={{0,4},{4,8},{8,12},{12,16},{16,20},{20,24},{24,28},{28,0},{1,5},{5... | collective-permute-start | bytes 589832 | tf_op jit(solution)/shard_map/ppermute | solution.py:26
  53.5 7.8 %collective-permute-start.10 = (bf16[128,768]{1,0:T(8,128)(2,1)S(1)}, bf16[128,768]{1,0:T(8,128)(2,1)S(1)}, u32[]{:S(2)}, u32[]{:S(2)}) collective-permute-start(bf16[128,768]{1,0:T(8,128)(2,1)S(1)} %slice.33), channel_id=1, source_target_pairs={{0,28},{4,0},{8,4},{12,8},{16,12},{20,16},{24,20},{28,24},{1,29},{... | collective-permute-start | bytes 589832 | tf_op jit(solution)/shard_map/ppermute | solution.py:26
  63.1 2.3 %collective-permute-start.12 = (bf16[4,3,32,768]{3,2,1,0:T(8,128)(2,1)S(1)}, bf16[4,3,32,768]{3,2,1,0:T(8,128)(2,1)S(1)}, u32[]{:S(2)}, u32[]{:S(2)}) collective-permute-start(bf16[4,3,32,768]{3,2,1,0:T(8,128)(2,1)S(1)} %get-tuple-element.97), channel_id=1, source_target_pairs={{0,32},{32,0},{1,33},{33,1},{2,34},{34,2},{3,35},{35,3},{4,36},{36... | collective-permute-start | bytes 1769480 | tf_op jit(solution)/shard_map/ppermute | solution.py:26
  65.5 7.4 %copy-start.6 = (bf16[256,768]{1,0:T(8,128)(2,1)S(1)}, bf16[256,768]{1,0:T(8,128)(2,1)}, u32[]{:S(2)}) copy-start(bf16[256,768]{1,0:T(8,128)(2,1)} %copy-done.5) | copy-start | bytes 1179652
  67.2 13.7 %collective-permute-start.13 = (bf16[8,32,768]{2,1,0:T(8,128)(2,1)}, bf16[8,32,768]{2,1,0:T(8,128)(2,1)}, u32[]{:S(2)}, u32[]{:S(2)}) collective-permute-start(bf16[8,32,768]{2,1,0:T(8,128)(2,1)} %get-tuple-element.99), channel_id=1, source_target_pairs={{0,64},{64,128},{128,192},{192,0},{1,65},{65,129},{129,193},{193,1... | collective-permute-start | bytes 1179656 | tf_op jit(solution)/shard_map/ppermute | solution.py:26
  68.7 20.7 %collective-permute-start.14 = (bf16[8,32,768]{2,1,0:T(8,128)(2,1)}, bf16[8,32,768]{2,1,0:T(8,128)(2,1)}, u32[]{:S(2)}, u32[]{:S(2)}) collective-permute-start(bf16[8,32,768]{2,1,0:T(8,128)(2,1)} %get-tuple-element.100), channel_id=1, source_target_pairs={{0,128},{64,192},{128,0},{192,64},{1,129},{65,193},{129,1},{193,65... | collective-permute-start | bytes 1179656 | tf_op jit(solution)/shard_map/ppermute | solution.py:26
  71.5 17.9 %collective-permute-start.15 = (bf16[8,32,768]{2,1,0:T(8,128)(2,1)}, bf16[8,32,768]{2,1,0:T(8,128)(2,1)}, u32[]{:S(2)}, u32[]{:S(2)}) collective-permute-start(bf16[8,32,768]{2,1,0:T(8,128)(2,1)} %get-tuple-element.101), channel_id=1, source_target_pairs={{0,192},{64,0},{128,64},{192,128},{1,193},{65,1},{129,65},{193,129... | collective-permute-start | bytes 1179656 | tf_op jit(solution)/shard_map/ppermute | solution.py:26
  72.9 1.9 copy-start
  74.8 14.6 %copy-start.1 = (bf16[2048,768]{1,0:T(8,128)(2,1)S(1)}, bf16[2048,768]{1,0:T(8,128)(2,1)}, u32[]{:S(2)}) copy-start(bf16[2048,768]{1,0:T(8,128)(2,1)} %all-gather.3.cloned.1.call-done.hid_ref) | copy-start | bytes 9437188
  91.3 17.3 %copy-start.3 = (bf16[768,768]{1,0:T(8,128)(2,1)S(1)}, bf16[768,768]{1,0:T(8,128)(2,1)}, u32[]{:S(2)}) copy-start(bf16[768,768]{1,0:T(8,128)(2,1)} %w_ref.3) | copy-start | bytes 3538948
  91.3 10.8 %collective-permute-start.16 = (bf16[4,32,768]{2,1,0:T(8,128)(2,1)S(1)}, bf16[4,32,768]{2,1,0:T(8,128)(2,1)S(1)}, u32[]{:S(2)}, u32[]{:S(2)}) collective-permute-start(bf16[4,32,768]{2,1,0:T(8,128)(2,1)S(1)} %get-tuple-element.106.refs_0_), channel_id=1, source_target_pairs={{0,192},{64,0},{128,64},{192,128},{1,193},{65,1},{129,65},{193,129... | collective-permute-start | bytes 589832 | tf_op jit(solution)/shard_map/ppermute | solution.py:26
  93.6 9.3 %collective-permute-start.17 = (bf16[4,32,768]{2,1,0:T(8,128)(2,1)S(1)}, bf16[4,32,768]{2,1,0:T(8,128)(2,1)S(1)}, u32[]{:S(2)}, u32[]{:S(2)}) collective-permute-start(bf16[4,32,768]{2,1,0:T(8,128)(2,1)S(1)} %get-tuple-element.106.refs_0_), channel_id=1, source_target_pairs={{0,128},{64,192},{128,0},{192,64},{1,129},{65,193},{129,1},{193,65... | collective-permute-start | bytes 589832 | tf_op jit(solution)/shard_map/ppermute | solution.py:26
  94.7 11.0 %collective-permute-start.18 = (bf16[4,32,768]{2,1,0:T(8,128)(2,1)S(1)}, bf16[4,32,768]{2,1,0:T(8,128)(2,1)S(1)}, u32[]{:S(2)}, u32[]{:S(2)}) collective-permute-start(bf16[4,32,768]{2,1,0:T(8,128)(2,1)S(1)} %get-tuple-element.106.refs_0_), channel_id=1, source_target_pairs={{0,64},{64,128},{128,192},{192,0},{1,65},{65,129},{129,193},{193,1... | collective-permute-start | bytes 589832 | tf_op jit(solution)/shard_map/ppermute | solution.py:26
  106.3 2.4 %collective-permute-start.19 = (bf16[4,4,32,768]{3,2,1,0:T(8,128)(2,1)S(1)}, bf16[4,4,32,768]{3,2,1,0:T(8,128)(2,1)S(1)}, u32[]{:S(2)}, u32[]{:S(2)}) collective-permute-start(bf16[4,4,32,768]{3,2,1,0:T(8,128)(2,1)S(1)} %stack_pre.2.ours_ref), channel_id=1, source_target_pairs={{0,32},{32,0},{1,33},{33,1},{2,34},{34,2},{3,35},{35,3},{4,36},{36... | collective-permute-start | bytes 2359304 | tf_op jit(solution)/shard_map/ppermute | solution.py:26
  110.6 29.1 %collective-permute-start.23 = (bf16[4,64,768]{2,1,0:T(8,128)(2,1)S(1)}, bf16[4,64,768]{2,1,0:T(8,128)(2,1)S(1)}, u32[]{:S(2)}, u32[]{:S(2)}) collective-permute-start(bf16[4,64,768]{2,1,0:T(8,128)(2,1)S(1)} %get-tuple-element.116), channel_id=1, source_target_pairs={{0,1},{1,2},{2,3},{3,0},{4,5},{5,6},{6,7},{7,4},{8,9},{9,10},{10,1... | collective-permute-start | bytes 1179656 | tf_op jit(solution)/shard_map/ppermute | solution.py:26
  112.3 27.5 %collective-permute-start.24 = (bf16[4,64,768]{2,1,0:T(8,128)(2,1)S(1)}, bf16[4,64,768]{2,1,0:T(8,128)(2,1)S(1)}, u32[]{:S(2)}, u32[]{:S(2)}) collective-permute-start(bf16[4,64,768]{2,1,0:T(8,128)(2,1)S(1)} %get-tuple-element.117), channel_id=1, source_target_pairs={{0,3},{1,0},{2,1},{3,2},{4,7},{5,4},{6,5},{7,6},{8,11},{9,8},{10,9... | collective-permute-start | bytes 1179656 | tf_op jit(solution)/shard_map/ppermute | solution.py:26
  117.3 17.5 %collective-permute-start.20 = (bf16[4,32,768]{2,1,0:T(8,128)(2,1)S(1)}, bf16[4,32,768]{2,1,0:T(8,128)(2,1)S(1)}, u32[]{:S(2)}, u32[]{:S(2)}) collective-permute-start(bf16[4,32,768]{2,1,0:T(8,128)(2,1)S(1)} %get-tuple-element.115.refs_0_), channel_id=1, source_target_pairs={{0,192},{64,0},{128,64},{192,128},{1,193},{65,1},{129,65},{193,129... | collective-permute-start | bytes 589832 | tf_op jit(solution)/shard_map/ppermute | solution.py:26
  127.6 9.4 %collective-permute-start.21 = (bf16[4,32,768]{2,1,0:T(8,128)(2,1)S(1)}, bf16[4,32,768]{2,1,0:T(8,128)(2,1)S(1)}, u32[]{:S(2)}, u32[]{:S(2)}) collective-permute-start(bf16[4,32,768]{2,1,0:T(8,128)(2,1)S(1)} %get-tuple-element.115.refs_0_), channel_id=1, source_target_pairs={{0,128},{64,192},{128,0},{192,64},{1,129},{65,193},{129,1},{193,65... | collective-permute-start | bytes 589832 | tf_op jit(solution)/shard_map/ppermute | solution.py:26
  128.3 11.4 %collective-permute-start.22 = (bf16[4,32,768]{2,1,0:T(8,128)(2,1)S(1)}, bf16[4,32,768]{2,1,0:T(8,128)(2,1)S(1)}, u32[]{:S(2)}, u32[]{:S(2)}) collective-permute-start(bf16[4,32,768]{2,1,0:T(8,128)(2,1)S(1)} %get-tuple-element.115.refs_0_), channel_id=1, source_target_pairs={{0,64},{64,128},{128,192},{192,0},{1,65},{65,129},{129,193},{193,1... | collective-permute-start | bytes 589832 | tf_op jit(solution)/shard_map/ppermute | solution.py:26
  140.3 2.4 %collective-permute-start.25 = (bf16[4,4,32,768]{3,2,1,0:T(8,128)(2,1)S(1)}, bf16[4,4,32,768]{3,2,1,0:T(8,128)(2,1)S(1)}, u32[]{:S(2)}, u32[]{:S(2)}) collective-permute-start(bf16[4,4,32,768]{3,2,1,0:T(8,128)(2,1)S(1)} %stack_pre.3.ours_ref), channel_id=1, source_target_pairs={{0,32},{32,0},{1,33},{33,1},{2,34},{34,2},{3,35},{35,3},{4,36},{36... | collective-permute-start | bytes 2359304 | tf_op jit(solution)/shard_map/ppermute | solution.py:26
  140.4 13.0 %collective-permute-start.26 = (bf16[4,64,768]{2,1,0:T(8,128)(2,1)S(1)}, bf16[4,64,768]{2,1,0:T(8,128)(2,1)S(1)}, u32[]{:S(2)}, u32[]{:S(2)}) collective-permute-start(bf16[4,64,768]{2,1,0:T(8,128)(2,1)S(1)} %get-tuple-element.128), channel_id=1, source_target_pairs={{0,2},{1,3},{2,0},{3,1},{4,6},{5,7},{6,4},{7,5},{8,10},{9,11},{10,... | collective-permute-start | bytes 1179656 | tf_op jit(solution)/shard_map/ppermute | solution.py:26
  144.7 21.7 %copy-start.7 = (f32[4,64,768]{2,1,0:T(8,128)}, f32[4,64,768]{2,1,0:T(8,128)S(1)}, u32[]{:S(2)}) copy-start(f32[4,64,768]{2,1,0:T(8,128)S(1)} %get-tuple-element.124) | copy-start | bytes 2359300
  153.7 11.9 %collective-permute-start.29 = (bf16[4,64,768]{2,1,0:T(8,128)(2,1)S(1)}, bf16[4,64,768]{2,1,0:T(8,128)(2,1)S(1)}, u32[]{:S(2)}, u32[]{:S(2)}) collective-permute-start(bf16[4,64,768]{2,1,0:T(8,128)(2,1)S(1)} %get-tuple-element.138), channel_id=1, source_target_pairs={{0,1},{1,2},{2,3},{3,0},{4,5},{5,6},{6,7},{7,4},{8,9},{9,10},{10,1... | collective-permute-start | bytes 1179656 | tf_op jit(solution)/shard_map/ppermute | solution.py:26
  154.8 10.7 %collective-permute-start.30 = (bf16[4,64,768]{2,1,0:T(8,128)(2,1)S(1)}, bf16[4,64,768]{2,1,0:T(8,128)(2,1)S(1)}, u32[]{:S(2)}, u32[]{:S(2)}) collective-permute-start(bf16[4,64,768]{2,1,0:T(8,128)(2,1)S(1)} %get-tuple-element.139), channel_id=1, source_target_pairs={{0,3},{1,0},{2,1},{3,2},{4,7},{5,4},{6,5},{7,6},{8,11},{9,8},{10,9... | collective-permute-start | bytes 1179656 | tf_op jit(solution)/shard_map/ppermute | solution.py:26
  156.7 5.8 %collective-permute-start.27 = (bf16[64,768]{1,0:T(8,128)(2,1)S(1)}, bf16[64,768]{1,0:T(8,128)(2,1)S(1)}, u32[]{:S(2)}, u32[]{:S(2)}) collective-permute-start(bf16[64,768]{1,0:T(8,128)(2,1)S(1)} %get-tuple-element.136), channel_id=1, source_target_pairs={{0,4},{4,8},{8,12},{12,16},{16,20},{20,24},{24,28},{28,0},{1,5},{5... | collective-permute-start | bytes 294920 | tf_op jit(solution)/shard_map/ppermute | solution.py:26
  156.7 5.8 %collective-permute-start.28 = (bf16[64,768]{1,0:T(8,128)(2,1)S(1)}, bf16[64,768]{1,0:T(8,128)(2,1)S(1)}, u32[]{:S(2)}, u32[]{:S(2)}) collective-permute-start(bf16[64,768]{1,0:T(8,128)(2,1)S(1)} %get-tuple-element.137), channel_id=1, source_target_pairs={{0,28},{4,0},{8,4},{12,8},{16,12},{20,16},{24,20},{28,24},{1,29},{... | collective-permute-start | bytes 294920 | tf_op jit(solution)/shard_map/ppermute | solution.py:26
  165.5 5.5 %copy-start.9 = (bf16[4,64,768]{2,1,0:T(8,128)(2,1)}, bf16[4,64,768]{2,1,0:T(8,128)(2,1)S(1)}, u32[]{:S(2)}) copy-start(bf16[4,64,768]{2,1,0:T(8,128)(2,1)S(1)} %collective-permute-done.29) | copy-start | bytes 1179652
  165.5 5.5 %copy-start.11 = (bf16[4,64,768]{2,1,0:T(8,128)(2,1)}, bf16[4,64,768]{2,1,0:T(8,128)(2,1)S(1)}, u32[]{:S(2)}) copy-start(bf16[4,64,768]{2,1,0:T(8,128)(2,1)S(1)} %collective-permute-done.30) | copy-start | bytes 1179652
  166.3 14.5 %collective-permute-start.33 = (bf16[4,64,768]{2,1,0:T(8,128)(2,1)S(1)}, bf16[4,64,768]{2,1,0:T(8,128)(2,1)}, u32[]{:S(2)}, u32[]{:S(2)}) collective-permute-start(bf16[4,64,768]{2,1,0:T(8,128)(2,1)S(1)} %get-tuple-element.146), channel_id=1, source_target_pairs={{0,2},{1,3},{2,0},{3,1},{4,6},{5,7},{6,4},{7,5},{8,10},{9,11},{10,... | collective-permute-start | bytes 1179656 | tf_op jit(solution)/shard_map/ppermute | solution.py:26
  171.1 9.8 %collective-permute-start.31 = (bf16[64,768]{1,0:T(8,128)(2,1)}, bf16[64,768]{1,0:T(8,128)(2,1)}, u32[]{:S(2)}, u32[]{:S(2)}) collective-permute-start(bf16[64,768]{1,0:T(8,128)(2,1)} %get-tuple-element.144), channel_id=1, source_target_pairs={{0,4},{4,8},{8,12},{12,16},{16,20},{20,24},{24,28},{28,0},{1,5},{5... | collective-permute-start | bytes 294920 | tf_op jit(solution)/shard_map/ppermute | solution.py:26
  171.1 9.8 %collective-permute-start.32 = (bf16[64,768]{1,0:T(8,128)(2,1)}, bf16[64,768]{1,0:T(8,128)(2,1)}, u32[]{:S(2)}, u32[]{:S(2)}) collective-permute-start(bf16[64,768]{1,0:T(8,128)(2,1)} %get-tuple-element.145), channel_id=1, source_target_pairs={{0,28},{4,0},{8,4},{12,8},{16,12},{20,16},{24,20},{28,24},{1,29},{... | collective-permute-start | bytes 294920 | tf_op jit(solution)/shard_map/ppermute | solution.py:26
  174.3 1.9 copy-start.4
  176.2 4.7 %copy-start.8 = (f32[4,64,768]{2,1,0:T(8,128)S(1)}, f32[4,64,768]{2,1,0:T(8,128)}, u32[]{:S(2)}) copy-start(f32[4,64,768]{2,1,0:T(8,128)} %copy-done.7) | copy-start | bytes 2359300
  176.2 4.7 %copy-start.10 = (bf16[4,64,768]{2,1,0:T(8,128)(2,1)S(1)}, bf16[4,64,768]{2,1,0:T(8,128)(2,1)}, u32[]{:S(2)}) copy-start(bf16[4,64,768]{2,1,0:T(8,128)(2,1)} %copy-done.9) | copy-start | bytes 1179652
  176.2 4.7 %copy-start.12 = (bf16[4,64,768]{2,1,0:T(8,128)(2,1)S(1)}, bf16[4,64,768]{2,1,0:T(8,128)(2,1)}, u32[]{:S(2)}) copy-start(bf16[4,64,768]{2,1,0:T(8,128)(2,1)} %copy-done.11) | copy-start | bytes 1179652
  183.1 5.9 %collective-permute-start.34 = (bf16[64,768]{1,0:T(8,128)(2,1)S(1)}, bf16[64,768]{1,0:T(8,128)(2,1)S(1)}, u32[]{:S(2)}, u32[]{:S(2)}) collective-permute-start(bf16[64,768]{1,0:T(8,128)(2,1)S(1)} %get-tuple-element.155), channel_id=1, source_target_pairs={{0,4},{4,8},{8,12},{12,16},{16,20},{20,24},{24,28},{28,0},{1,5},{5... | collective-permute-start | bytes 294920 | tf_op jit(solution)/shard_map/ppermute | solution.py:26
  183.1 5.8 %collective-permute-start.35 = (bf16[64,768]{1,0:T(8,128)(2,1)S(1)}, bf16[64,768]{1,0:T(8,128)(2,1)S(1)}, u32[]{:S(2)}, u32[]{:S(2)}) collective-permute-start(bf16[64,768]{1,0:T(8,128)(2,1)S(1)} %get-tuple-element.156), channel_id=1, source_target_pairs={{0,28},{4,0},{8,4},{12,8},{16,12},{20,16},{24,20},{28,24},{1,29},{... | collective-permute-start | bytes 294920 | tf_op jit(solution)/shard_map/ppermute | solution.py:26
  189.0 5.9 %collective-permute-start.36 = (bf16[64,768]{1,0:T(8,128)(2,1)S(1)}, bf16[64,768]{1,0:T(8,128)(2,1)S(1)}, u32[]{:S(2)}, u32[]{:S(2)}) collective-permute-start(bf16[64,768]{1,0:T(8,128)(2,1)S(1)} %fusion.1), channel_id=1, source_target_pairs={{0,4},{4,8},{8,12},{12,16},{16,20},{20,24},{24,28},{28,0},{1,5},{5... | collective-permute-start | bytes 294920 | tf_op jit(solution)/shard_map/ppermute | solution.py:26
Sparse Core Ops, SparseCore 0:
  9.8 33.1 all-gather.2
  45.6 78.7 all-gather.4
